TPU v7x, 32 devices: a whole 2x2x4 slice. The times are simulated.
32 devices in a mesh: shards: 2 (over x), tensor: 4 (over y, core), replica: 4 (over z).
Axes of the slice: x: 2, y: 2, z: 4, core: 2. Of those that a mesh axis runs over, the one named last changes fastest.
Arguments:
- activations: bfloat16 [32768, 1024], P(('shards', 'tensor', 'replica')), may hold values from -6 to 6
- grads_out: bfloat16 [32768, 1024], P(('shards', 'tensor', 'replica')), may hold values from -6 to 6
- grad_parts: float32 [8, 1024, 1024], P(('shards', 'replica'), None, 'tensor'), may hold values from -80 to 80
- old_factors: float32 [16, 128, 128], replicated, may hold values from -16 to 16, as said below
- block_owner: int32 [16], replicated, may hold values from 0 to 1, as said below
- weights: float32 [1024, 1024], P(('shards', 'replica'), 'tensor'), may hold values from -0.1875 to 0.1875
- momentum: float32 [1024, 1024], P(('shards', 'replica'), 'tensor'), may hold values from -4 to 4
Outputs:
- weights_next: float32 [1024, 1024], P(None, 'tensor')
- momentum_next: float32 [1024, 1024], P(('shards', 'replica'), 'tensor')
- next_factor_blocks: float32 [18, 128, 128], P('shards')
Inputs may be any that keep to these rules, and one draw needn't show every extreme that they name: `block_owner`: each shard index owns at most 9 of the 16 blocks, and some index owns exactly 9. `old_factors`: each block is symmetric and positive definite.
All inputs are finite; a program needn't handle non-finite values. Where the computation divides by a largest or mean magnitude, that divisor is 1e-20 or more.
Results may differ from a plain program's by a relative error of at most 0.0003.
Values sent between devices are 32-bit elements; how exact they have to be, the bound alone decides.
A program may use at most 64 MiB of HBM per device.

v0:
```python
import jax
import jax.numpy as jnp
from jax import lax
from jax.sharding import PartitionSpec as P

NS_STEPS = 4


exact_mode = lax.Precision.HIGHEST
decay_rate = 0.75
damping = 0.1
damp_shift = 0.001
clip_norm = 256.0
momentum_rate = 0.9
step_rate = 0.05


def sample_stats(samples, block_size):
    sample_rows, width = samples.shape
    blocks = samples.reshape(sample_rows, width // block_size, block_size)
    return jnp.einsum("tnb,tnc->nbc", blocks, blocks, preferred_element_type=jnp.float32)


def build_slots(block_owner, capacity, slot_count):
    block_count = block_owner.shape[0]
    positions = jnp.arange(block_count, dtype=jnp.int32)
    earlier = (block_owner[:, None] == block_owner[None, :]) & (
        positions[None, :] < positions[:, None]
    )
    owner_slot_list = block_owner * capacity + jnp.sum(earlier.astype(jnp.int32), axis=1)
    return (owner_slot_list[None, :] == jnp.arange(slot_count, dtype=jnp.int32)[:, None]).astype(
        jnp.float32
    )


def newton_inverse(mixed_factor_blocks):
    block_size = mixed_factor_blocks.shape[-1]
    identity = jnp.eye(block_size, dtype=jnp.float32)
    traces = jnp.trace(mixed_factor_blocks, axis1=1, axis2=2)
    damped = (
        mixed_factor_blocks + (damping * traces / block_size + damp_shift)[:, None, None] * identity
    )
    bounds = jnp.max(jnp.sum(jnp.abs(damped), axis=2), axis=1)
    approx = identity[None, :, :] / bounds[:, None, None]
    for iteration in range(NS_STEPS):
        left_part = jnp.einsum("nab,nbc->nac", approx, damped, precision=exact_mode)
        approx = 2.0 * approx - jnp.einsum("nab,nbc->nac", left_part, approx, precision=exact_mode)
    return approx


def apply_right(left_part, right_inv, block_size):
    row_count, col_count = left_part.shape
    right_count = col_count // block_size
    return jnp.einsum(
        "rnb,nbc->rnc",
        left_part.reshape(row_count, right_count, block_size),
        right_inv,
        precision=exact_mode,
    ).reshape(row_count, col_count)


def body(activations, grads_out, grad_parts, old_factors, block_owner, weights, momentum):
    shard_count = lax.axis_size("shards")
    block_count = old_factors.shape[0]
    block_size = old_factors.shape[1]
    capacity = (block_count + shard_count - 1) // shard_count + 1
    slot_count = capacity * shard_count
    slot_table = build_slots(block_owner, capacity, slot_count)
    local_stats = jnp.concatenate(
        [sample_stats(activations, block_size), sample_stats(grads_out, block_size)], axis=0
    )
    packed = jnp.dot(
        slot_table, local_stats.reshape(block_count, block_size * block_size), precision=exact_mode
    )
    first_slot = lax.axis_index("shards") * capacity
    summed = lax.psum(packed, ("shards", "tensor", "replica"))
    owned = lax.dynamic_slice_in_dim(summed, first_slot, capacity, 0)
    sample_count = (
        activations.shape[0] * shard_count * lax.axis_size("tensor") * lax.axis_size("replica")
    )
    owned_table = lax.dynamic_slice_in_dim(slot_table, first_slot, capacity, 0)
    old_owned = jnp.dot(
        owned_table, old_factors.reshape(block_count, block_size * block_size), precision=exact_mode
    )
    mixed_factor_blocks = (
        decay_rate * old_owned + (1.0 - decay_rate) * (owned / sample_count)
    ).reshape(capacity, block_size, block_size)
    inverse_owned = newton_inverse(mixed_factor_blocks)
    start_blocks = jnp.zeros((block_count, block_size * block_size), jnp.float32)
    shard_piece = lax.all_gather(inverse_owned, "shards", axis=0, tiled=True)
    piece_rows = shard_piece.shape[0]
    rows_table = lax.slice_in_dim(slot_table, 0, piece_rows, axis=0)
    flat_piece = shard_piece.reshape(piece_rows, block_size * block_size)
    inverse_flat = start_blocks + jnp.einsum(
        "sb,sk->bk", rows_table, flat_piece, precision=exact_mode
    )
    inverse_blocks = inverse_flat.reshape(block_count, block_size, block_size)
    partial_grad = grad_parts[0]
    row_count, col_count = partial_grad.shape
    left_count = row_count // block_size
    right_count = col_count // block_size
    right_first = left_count + lax.axis_index("tensor") * right_count
    right_inv = lax.dynamic_slice_in_dim(inverse_blocks, right_first, right_count, 0)
    left_part = jnp.einsum(
        "nab,nbc->nac",
        inverse_blocks[:left_count],
        partial_grad.reshape(left_count, block_size, col_count),
        precision=exact_mode,
    ).reshape(row_count, col_count)
    precond = apply_right(left_part, right_inv, block_size)
    total_precond, total_grad = (
        lax.psum_scatter(precond, ("shards", "replica"), scatter_dimension=0, tiled=True),
        lax.psum_scatter(partial_grad, ("shards", "replica"), scatter_dimension=0, tiled=True),
    )
    alignment_sum = lax.psum(jnp.sum(total_precond * total_grad), ("shards", "tensor", "replica"))
    clip_scale = jnp.minimum(1.0, clip_norm / jnp.sqrt(alignment_sum))
    momentum_next = momentum_rate * momentum + clip_scale * total_precond
    weights_next = weights - step_rate * momentum_next
    gathered = lax.all_gather(weights_next, ("shards", "replica"), axis=0, tiled=True)
    return (gathered, momentum_next, mixed_factor_blocks)


def solution(mesh):
    placed = (
        P(("shards", "tensor", "replica"), None),
        P(("shards", "tensor", "replica"), None),
        P(("shards", "replica"), None, "tensor"),
        P(),
        P(),
        P(("shards", "replica"), "tensor"),
        P(("shards", "replica"), "tensor"),
    )
    return jax.shard_map(
        body,
        mesh=mesh,
        in_specs=placed,
        out_specs=(P(None, "tensor"), P(("shards", "replica"), "tensor"), P("shards", None, None)),
        check_vma=False,
    )
```

profile of v0, /device:TPU:0, one launch (start us, length us, event | category | flops | bytes accessed | tf_op | source)
XLA Modules:
  0.0 397.3 jit_solution(1371889030548616770)
XLA Ops:
  8.1 1.0 convert_reduce_fusion
  9.1 0.9 multiply_add_fusion.7
  10.0 1.1 fusion.1
  11.0 1.1 fusion.4
  12.3 2.5 fusion.7
  15.1 134.7 %all-reduce.2.cloned.1.call-done = f32[18,16384]{1,0:T(8,128)} async-done(((f32[18,16384]{1,0:T(8,128)}), f32[18,16384]{1,0:T(8,128)}) %all-reduce.2.cloned.1.call-update) | async-done | bytes 1179664 | tf_op jit(solution)/shard_map/psum | solution.py:76
  149.8 3.0 select_reduce_fusion
  153.4 0.8 fusion.14
  154.3 0.7 convolution_subtract_fusion.3
  155.0 0.8 fusion.21
  155.8 0.7 convolution_subtract_fusion.2
  156.5 0.8 fusion.20
  157.3 0.7 convolution_subtract_fusion.1
  158.0 0.8 fusion.19
  158.7 1.5 convolution_subtract_fusion
  160.3 0.5 reduce-scatter.5.cloned.1.call-update
  161.1 21.1 %all-gather.3.cloned.1.call-done = f32[18,128,128]{2,1,0:T(8,128)} async-done(((f32[9,128,128]{2,1,0:T(8,128)}), f32[18,128,128]{2,1,0:T(8,128)}) %all-gather.3.cloned.1.call-update) | async-done | bytes 1179664 | tf_op jit(solution)/shard_map/all_gather | solution.py:90
  182.3 1.4 pad.2
  183.7 0.9 copy.40
  184.6 0.7 fusion.38
  185.9 2.0 fusion.17
  187.9 2.7 reshape_reshape.3
  190.8 1.0 copy-done.2
  191.9 1.1 fusion.12
  193.0 1.3 copy.33
  194.3 41.6 %reduce-scatter.5.cloned.1.call-done = f32[128,256]{1,0:T(8,128)} async-done(((f32[1024,256]{1,0:T(8,128)}), f32[128,256]{1,0:T(8,128)}) %reduce-scatter.5.cloned.1.call-update) | async-done | bytes 131088 | tf_op jit(solution)/shard_map/reduce_scatter | solution.py:113
  235.9 67.5 %reduce-scatter.3.cloned.1.call-done = f32[128,256]{1,0:T(8,128)} async-done(((f32[1024,256]{1,0:T(8,128)}), f32[128,256]{1,0:T(8,128)}) %reduce-scatter.3.cloned.1.call-update) | async-done | bytes 131088 | tf_op jit(solution)/shard_map/reduce_scatter | solution.py:112
  303.5 1.6 multiply_reduce_fusion
  305.1 40.3 %psum.15 = f32[]{:T(128)} all-reduce(f32[]{:T(128)} %multiply_reduce_fusion), channel_id=1, replica_groups=mesh['shards'=2,'tensor'=4,'replica'=4] {'shards','tensor','replica'}, use_global_device_ids=true, to_apply=%region_8.9 | all-reduce | flops 1 | bytes 8 | tf_op jit(solution)/shard_map/psum | solution.py:115
  346.1 1.6 multiply_subtract_fusion
  347.7 39.7 %all-gather.5.cloned.1.call-done = f32[1024,256]{1,0:T(8,128)} async-done(((f32[128,256]{1,0:T(8,128)}), f32[1024,256]{1,0:T(8,128)}) %all-gather.5.cloned.1.call-update) | async-done | bytes 1048592 | tf_op jit(solution)/shard_map/all_gather | solution.py:119
  387.4 2.3 copy.66
  (34 shorter events, 2.2 us)
Async XLA Ops:
  8.0 2.0 copy-start
  8.0 141.8 %all-reduce.2.cloned.1.call-start = ((), (), s32[]{:S(2)}) async-start(), calls=%async_computation.2 | async-start | bytes 3145728 | tf_op jit(solution)/shard_map/psum | solution.py:76
  8.1 3.0 copy-start.7
  12.2 137.5 %copy-start.4 = (f32[16,128,128]{2,1,0:T(8,128)S(1)}, f32[16,128,128]{2,1,0:T(8,128)}, u32[]{:S(2)}) copy-start(f32[16,128,128]{2,1,0:T(8,128)} %param.10) | copy-start | bytes 3145732
  14.8 167.5 %all-gather.3.cloned.1.call-start = ((), (), s32[]{:S(2)}) async-start(), calls=%async_computation.3 | async-start | bytes 1769472 | tf_op jit(solution)/shard_map/all_gather | solution.py:90
  153.3 4.7 %copy-start.1 = (f32[9,128,128]{2,1,0:T(8,128)}, f32[9,128,128]{2,1,0:T(8,128)S(1)}, u32[]{:S(2)}) copy-start(f32[9,128,128]{2,1,0:T(8,128)S(1)} %get-tuple-element.14) | copy-start | bytes 1769476
  160.3 75.6 %reduce-scatter.5.cloned.1.call-start = ((), (), s32[]{:S(2)}) async-start(), calls=%async_computation.5 | async-start | bytes 1179648 | tf_op jit(solution)/shard_map/reduce_scatter | solution.py:113
  160.9 142.6 %reduce-scatter.3.cloned.1.call-start = ((), (), s32[]{:S(2)}) async-start(), calls=%async_computation.4 | async-start | bytes 1179648 | tf_op jit(solution)/shard_map/reduce_scatter | solution.py:112
  184.6 1.2 copy-start.3
  190.6 1.2 copy-start.2
  192.9 153.1 %copy-start.5 = (f32[128,256]{1,0:T(8,128)S(1)}, f32[128,256]{1,0:T(8,128)}, u32[]{:S(2)}) copy-start(f32[128,256]{1,0:T(8,128)} %param.12) | copy-start | bytes 393220
  192.9 153.1 %copy-start.6 = (f32[128,256]{1,0:T(8,128)S(1)}, f32[128,256]{1,0:T(8,128)}, u32[]{:S(2)}) copy-start(f32[128,256]{1,0:T(8,128)} %param.13) | copy-start | bytes 393220
  194.3 193.1 %all-gather.5.cloned.1.call-start = ((), (), s32[]{:S(2)}) async-start(), calls=%async_computation.6 | async-start | bytes 1179648 | tf_op jit(solution)/shard_map/all_gather | solution.py:119
Sparse Core Ops, SparseCore 0:
  15.0 134.7 all-reduce.1
  160.4 21.8 all-gather.2
Sparse Core Ops, SparseCore 1:
  164.2 71.7 reduce-scatter.4
  240.2 63.2 reduce-scatter.2
  347.8 39.5 all-gather.4
where the time goes:
time: 398 us; the launch traced here: 397 us
  waiting for transfers between devices  305 us (77%)
  blocking collectives  40.3 us (10%)
  matrix products  18.2 us (5%)
  between operations  16.6 us (4%)
  local copies, waits for them, and re-layouts  10.6 us (3%)
  other arithmetic  5.67 us (1%)
    psum x1, waiting for transfers between devices, body(): summed = lax.psum(packed, ('shards', 'tensor', 'replica'))  135 us
    reduce_scatter x1, waiting for transfers between devices, body(): lax.psum_scatter(precond, ('shards', 'replica'), scatter_dimension=0, til...  67.5 us
    reduce_scatter x1, waiting for transfers between devices, body(): lax.psum_scatter(partial_grad, ('shards', 'replica'), scatter_dimension=0...  41.6 us
    psum x1, blocking collectives, body(): lax.psum(jnp.sum(total_precond * total_grad), ('shards', 'tensor', 'repli...  40.3 us
    all_gather x1, waiting for transfers between devices, body(): lax.all_gather(weights_next, ('shards', 'replica'), axis=0, tiled=True)  39.7 us
    all_gather x1, waiting for transfers between devices, body(): shard_piece = lax.all_gather(inverse_owned, 'shards', axis=0, tiled=True)  21.1 us
  transfers between devices with their start and end apart: 5, of which 5 were waited for; matrix products, arithmetic and copies ran while one was open for 3% of the time, Pallas kernels for 0%

commit v1 on v0

--- a/solution.py
+++ b/solution.py
@@ -1,7 +1,13 @@
+import functools
+
 import jax
 import jax.numpy as jnp
 from jax import lax
+from jax.experimental import pallas as pl
+from jax.experimental.pallas import tpu as pltpu
 from jax.sharding import PartitionSpec as P
+
+MESH = pl.DeviceIdType.MESH
 
 NS_STEPS = 4
 
@@ -120,6 +126,422 @@
     return (gathered, momentum_next, mixed_factor_blocks)
 
 
+def remote(src, dst, sends, recvs, index, device):
+    return pltpu.make_async_remote_copy(
+        src_ref=src,
+        dst_ref=dst,
+        send_sem=sends.at[index],
+        recv_sem=recvs.at[index],
+        device_id=device,
+        device_id_type=MESH,
+    )
+
+
+def unpack_pair(packed, diagonal, lower, on_diagonal):
+    flipped = packed.T
+    first = jnp.where(lower, flipped, packed)
+    second = jnp.where(lower, packed, jnp.where(on_diagonal, diagonal, flipped))
+    return first, second
+
+
+def dot_exact(a, b):
+    return jnp.dot(a, b, precision=exact_mode, preferred_element_type=jnp.float32)
+
+
+def fused_kernel(
+    sample_total,
+    owner_ref,
+    act_ref,
+    gout_ref,
+    grad_ref,
+    old_ref,
+    weights_ref,
+    momentum_ref,
+    weights_out,
+    momentum_out,
+    factors_out,
+    act_v,
+    gout_v,
+    packed_v,
+    core_in,
+    y_in,
+    z_out,
+    z_in,
+    x_out,
+    x_in,
+    full_v,
+    diag_out,
+    diag_in,
+    diag_z,
+    grad_own,
+    grad_x,
+    grad_z,
+    sum_out,
+    sum_xz,
+    sum_tensor,
+    new_weights,
+    mixed_v,
+    local_sem,
+    sends,
+    recvs,
+):
+    s = lax.axis_index("shards")
+    t = lax.axis_index("tensor")
+    r = lax.axis_index("replica")
+    y = t // 2
+    c = t % 2
+    n = 128
+    half = 512
+    quarter = 256
+    x_peer = (1 - s, t, r)
+    y_peer = (s, 2 * (1 - y) + c, r)
+    c_peer = (s, 2 * y + 1 - c, r)
+    yc_peer = (s, 2 * (1 - y) + 1 - c, r)
+    z_ranks = [(r + d) % 4 for d in (1, 2, 3)]
+    z_peers = [(s, t, q) for q in z_ranks]
+    xz_peers = [(1 - s, t, q) for q in z_ranks]
+
+    def part(ref, start, size):
+        return ref.at[pl.ds(pl.multiple_of(start, 8), size)]
+
+    loads = []
+    for k, core in enumerate((1 - c, c)):
+        columns = pl.ds(pl.multiple_of(core * half, half), half)
+        for src, dst in ((act_ref, act_v), (gout_ref, gout_v)):
+            copy = pltpu.make_async_copy(
+                src.at[:, columns], dst.at[:, columns], local_sem.at[len(loads)]
+            )
+            copy.start()
+            loads.append(copy)
+    own_load = pltpu.make_async_copy(
+        grad_ref.at[0, pl.ds(pl.multiple_of(s * half, half), half)], grad_own, local_sem.at[4]
+    )
+    own_load.start()
+
+    barrier = pltpu.get_barrier_semaphore()
+    peers = [x_peer, y_peer, c_peer, yc_peer] + z_peers + xz_peers
+    for peer in peers:
+        pl.semaphore_signal(barrier, inc=1, device_id=peer, device_id_type=MESH)
+    pl.semaphore_wait(barrier, len(peers))
+
+    count = 0
+    grad_x_copies = []
+    for k in range(4):
+        copy = remote(
+            grad_ref.at[0, pl.ds(pl.multiple_of((1 - s) * half + k * n, n), n)],
+            grad_x.at[k],
+            sends,
+            recvs,
+            count,
+            x_peer,
+        )
+        count += 1
+        copy.start()
+        grad_x_copies.append(copy)
+
+    rows = lax.broadcasted_iota(jnp.int32, (n, n), 0)
+    cols = lax.broadcasted_iota(jnp.int32, (n, n), 1)
+    lower = rows > cols
+    on_diagonal = rows == cols
+    pair_rows = lax.broadcasted_iota(jnp.int32, (8, n), 0)
+    identity = on_diagonal.astype(jnp.float32)
+
+    diag = jnp.zeros((8, n), jnp.float32)
+    core_copies = []
+    y_copy = None
+    for j, (core, side) in enumerate(((1 - c, 1 - y), (1 - c, y), (c, 1 - y), (c, y))):
+        if j % 2 == 0:
+            loads[j].wait()
+            loads[j + 1].wait()
+        start = pl.multiple_of(core * half + side * quarter, quarter)
+        columns = pl.ds(start, quarter)
+        a = act_v[:, columns]
+        g = gout_v[:, columns]
+        across = (((0,), (0,)), ((), ()))
+        left = lax.dot_general(a, a, across, preferred_element_type=jnp.float32)
+        right = lax.dot_general(g, g, across, preferred_element_type=jnp.float32)
+        for k in range(2):
+            span = slice(k * n, (k + 1) * n)
+            second = right[span, span]
+            packed_v[pl.ds(start + k * n, n), :] = jnp.where(lower, second, left[span, span])
+            row = jnp.sum(jnp.where(on_diagonal, second, 0.0), axis=0, keepdims=True)
+            diag = jnp.where(pair_rows == core * 4 + side * 2 + k, row, diag)
+        if j < 2:
+            copy = remote(
+                part(packed_v, start, quarter), core_in.at[j], sends, recvs, count, c_peer
+            )
+            count += 1
+            copy.start()
+            core_copies.append(copy)
+        elif j == 2:
+            core_copies[0].wait()
+            packed_v[pl.ds(start, quarter), :] += core_in[0]
+            y_copy = remote(part(packed_v, start, quarter), y_in, sends, recvs, count, y_peer)
+            count += 1
+            y_copy.start()
+    diag_out[0] = diag
+    copy = remote(diag_out.at[0], diag_in.at[0], sends, recvs, count, c_peer)
+    count += 1
+    copy.start()
+    core_copies[1].wait()
+    copy.wait()
+    diag = diag + diag_in[0]
+    diag_out[1] = diag
+    diag_copy = remote(diag_out.at[1], diag_in.at[1], sends, recvs, count, y_peer)
+    count += 1
+    diag_copy.start()
+    start = pl.multiple_of(c * half + y * quarter, quarter)
+    mine = packed_v[pl.ds(start, quarter), :] + core_in[1]
+    y_copy.wait()
+    z_out[...] = (mine + y_in[...]).reshape(4, 64, n)
+    z_copies = []
+    for d in range(3):
+        copy = remote(z_out.at[z_ranks[d]], z_in.at[r], sends, recvs, count, z_peers[d])
+        count += 1
+        copy.start()
+        z_copies.append(copy)
+    diag_copy.wait()
+    diag = diag + diag_in[1]
+    diag_out[2] = diag
+    for d in range(3):
+        copy = remote(diag_out.at[2], diag_z.at[r], sends, recvs, count, z_peers[d])
+        count += 1
+        copy.start()
+        z_copies.append(copy)
+    z_in[r] = z_out[r]
+    diag_z[r] = diag
+    for copy in z_copies:
+        copy.wait()
+    x_out[...] = (z_in[0] + z_in[1]) + (z_in[2] + z_in[3])
+    x_copy = remote(part(x_out, (1 - s) * 32, 32), x_in, sends, recvs, count, x_peer)
+    count += 1
+    x_copy.start()
+    diag = (diag_z[0] + diag_z[1]) + (diag_z[2] + diag_z[3])
+    diag_out[3] = diag
+    diag_copy = remote(diag_out.at[3], diag_in.at[2], sends, recvs, count, x_peer)
+    count += 1
+    diag_copy.start()
+    x_copy.wait()
+    z_base = c * half + y * quarter + r * 64
+    start = pl.multiple_of(z_base + s * 32, 32)
+    full_v[pl.ds(start, 32), :] = x_out[pl.ds(pl.multiple_of(s * 32, 32), 32), :] + x_in[...]
+    region = part(full_v, start, 32)
+    copy = remote(region, region, sends, recvs, count, x_peer)
+    count += 1
+    copy.start()
+    diag_copy.wait()
+    diag = diag + diag_in[2]
+    diag_out[4] = diag
+    copy.wait()
+    z_copies = []
+    region = part(full_v, z_base, 64)
+    for d in range(3):
+        copy = remote(region, region, sends, recvs, count, z_peers[d])
+        count += 1
+        copy.start()
+        z_copies.append(copy)
+    own_load.wait()
+    for copy in z_copies:
+        copy.wait()
+    region = part(full_v, c * half + y * quarter, quarter)
+    y_copy = remote(region, region, sends, recvs, count, y_peer)
+    count += 1
+    y_copy.start()
+    for k in range(4):
+        grad_x_copies[k].wait()
+        grad_x[k] = grad_x[k] + grad_own[pl.ds(k * n, n), :]
+    grad_copies = []
+    for d in range(3):
+        copy = remote(grad_x.at[z_ranks[d]], grad_z.at[r], sends, recvs, count, z_peers[d])
+        count += 1
+        copy.start()
+        grad_copies.append(copy)
+    grad_z[r] = grad_x[r]
+    y_copy.wait()
+    region = part(full_v, c * half, half)
+    copy = remote(region, region, sends, recvs, count, c_peer)
+    count += 1
+    copy.start()
+    copy.wait()
+
+    def blend(pair):
+        first, second = unpack_pair(
+            full_v[pl.ds(pl.multiple_of(pair * n, n), n), :],
+            diag_out[4, pl.ds(pair, 1), :],
+            lower,
+            on_diagonal,
+        )
+        return (
+            decay_rate * old_ref[pair] + (1.0 - decay_rate) * (first / sample_total),
+            decay_rate * old_ref[8 + pair] + (1.0 - decay_rate) * (second / sample_total),
+        )
+
+    mixed = [blend(s * 4 + r)[0], blend(2 * t)[1], blend(2 * t + 1)[1]]
+    scales, rests = [], []
+    for block in mixed:
+        trace = jnp.sum(jnp.where(on_diagonal, block, 0.0), keepdims=True)
+        damped = block + (damping * trace / n + damp_shift) * identity
+        bound = jnp.max(
+            jnp.sum(jnp.abs(damped), axis=1, keepdims=True), axis=0, keepdims=True
+        )
+        scales.append(1.0 / bound)
+        rests.append(identity - damped / bound)
+    inverses = [identity + rest for rest in rests]
+    for _ in range(NS_STEPS - 1):
+        rests = [dot_exact(rest, rest) for rest in rests]
+        inverses = [inv + dot_exact(inv, rest) for inv, rest in zip(inverses, rests)]
+    inverses = [inv * scale for inv, scale in zip(inverses, scales)]
+
+    for copy in grad_copies:
+        copy.wait()
+    gradient = (grad_z[0] + grad_z[1]) + (grad_z[2] + grad_z[3])
+    left = dot_exact(inverses[0], gradient)
+    precond = jnp.concatenate(
+        [dot_exact(left[:, :n], inverses[1]), dot_exact(left[:, n:], inverses[2])], axis=1
+    )
+    products = precond * gradient
+    products = products[:, :n] + products[:, n:]
+    tile = jnp.sum(products.reshape(16, 8, n), axis=0)
+
+    place = s * 4 + r
+    sum_out[0] = tile
+    sum_copies = []
+    for peer in [x_peer] + z_peers + xz_peers:
+        copy = remote(sum_out.at[0], sum_xz.at[place], sends, recvs, count, peer)
+        count += 1
+        copy.start()
+        sum_copies.append(copy)
+    sum_xz[place] = tile
+    for copy in sum_copies:
+        copy.wait()
+    tile = jnp.sum(sum_xz[...], axis=0)
+    sum_out[1] = tile
+    sum_copies = []
+    for peer in (c_peer, y_peer, yc_peer):
+        copy = remote(sum_out.at[1], sum_tensor.at[t], sends, recvs, count, peer)
+        count += 1
+        copy.start()
+        sum_copies.append(copy)
+    sum_tensor[t] = tile
+    for copy in sum_copies:
+        copy.wait()
+    alignment = jnp.sum(jnp.sum(sum_tensor[...], axis=0), keepdims=True)
+    clip_scale = jnp.minimum(1.0, clip_norm / jnp.sqrt(alignment))
+    momentum_next = momentum_rate * momentum_ref[...] + clip_scale * precond
+    momentum_out[...] = momentum_next
+    new_weights[...] = weights_ref[...] - step_rate * momentum_next
+
+    target = part(weights_out, place * n, n)
+    own_store = pltpu.make_async_copy(new_weights, target, local_sem.at[5])
+    own_store.start()
+    gather = []
+    for peer in z_peers + [x_peer]:
+        copy = remote(new_weights, target, sends, recvs, count, peer)
+        count += 1
+        copy.start()
+        gather.append(copy)
+
+    for pair in range(8):
+        mixed_v[pair], mixed_v[8 + pair] = blend(pair)
+    mixed_v[16] = jnp.zeros((n, n), jnp.float32)
+    block_total = owner_ref.shape[0]
+    chosen = [jnp.int32(block_total)] * factors_out.shape[0]
+    used = jnp.int32(0)
+    for b in range(block_total):
+        here = owner_ref[b] == s
+        for k in range(min(b + 1, len(chosen))):
+            chosen[k] = jnp.where(here & (used == k), jnp.int32(b), chosen[k])
+        used = used + jnp.where(here, jnp.int32(1), jnp.int32(0))
+    for k in range(len(chosen)):
+        factors_out[k] = mixed_v[chosen[k]]
+
+    for d in range(3):
+        gather[d].wait()
+        origin = s * 4 + (r + 3 - d) % 4
+        region = part(weights_out, origin * n, n)
+        copy = remote(region, region, sends, recvs, count, x_peer)
+        count += 1
+        copy.start()
+        gather.append(copy)
+    for copy in gather[3:]:
+        copy.wait()
+    own_store.wait()
+
+
+def fused_step(activations, grads_out, grad_parts, old_factors, block_owner, weights, momentum):
+    n = old_factors.shape[1]
+    shards = lax.axis_size("shards")
+    capacity = (old_factors.shape[0] + shards - 1) // shards + 1
+    devices = shards * lax.axis_size("tensor") * lax.axis_size("replica")
+    f32 = jnp.float32
+    anywhere = pl.BlockSpec(memory_space=pl.ANY)
+    vmem = pl.BlockSpec(memory_space=pltpu.VMEM)
+    return pl.pallas_call(
+        functools.partial(fused_kernel, float(activations.shape[0] * devices)),
+        out_shape=(
+            jax.ShapeDtypeStruct(grad_parts.shape[1:], f32),
+            jax.ShapeDtypeStruct(momentum.shape, f32),
+            jax.ShapeDtypeStruct((capacity, n, n), f32),
+        ),
+        in_specs=[
+            pl.BlockSpec(memory_space=pltpu.SMEM),
+            anywhere,
+            anywhere,
+            anywhere,
+            vmem,
+            vmem,
+            vmem,
+        ],
+        out_specs=(anywhere, vmem, vmem),
+        scratch_shapes=[
+            pltpu.VMEM(activations.shape, activations.dtype),
+            pltpu.VMEM(grads_out.shape, grads_out.dtype),
+            pltpu.VMEM((1024, n), f32),
+            pltpu.VMEM((2, 256, n), f32),
+            pltpu.VMEM((256, n), f32),
+            pltpu.VMEM((4, 64, n), f32),
+            pltpu.VMEM((4, 64, n), f32),
+            pltpu.VMEM((64, n), f32),
+            pltpu.VMEM((32, n), f32),
+            pltpu.VMEM((1024, n), f32),
+            pltpu.VMEM((5, 8, n), f32),
+            pltpu.VMEM((3, 8, n), f32),
+            pltpu.VMEM((4, 8, n), f32),
+            pltpu.VMEM((512, 256), f32),
+            pltpu.VMEM((4, n, 256), f32),
+            pltpu.VMEM((4, n, 256), f32),
+            pltpu.VMEM((2, 8, n), f32),
+            pltpu.VMEM((8, 8, n), f32),
+            pltpu.VMEM((4, 8, n), f32),
+            pltpu.VMEM((n, 256), f32),
+            pltpu.VMEM((17, n, n), f32),
+            pltpu.SemaphoreType.DMA((6,)),
+            pltpu.SemaphoreType.DMA((48,)),
+            pltpu.SemaphoreType.DMA((48,)),
+        ],
+        compiler_params=pltpu.CompilerParams(
+            collective_id=0, has_side_effects=True, vmem_limit_bytes=40 * 1024 * 1024
+        ),
+        cost_estimate=pl.CostEstimate(
+            flops=1_200_000_000, bytes_accessed=10_000_000, transcendentals=0
+        ),
+    )(block_owner, activations, grads_out, grad_parts, old_factors, weights, momentum)
+
+
+def step(activations, grads_out, grad_parts, old_factors, block_owner, weights, momentum):
+    sizes = tuple(lax.axis_size(name) for name in ("shards", "tensor", "replica"))
+    fits = (
+        sizes == (2, 4, 4)
+        and weights.shape == (128, 256)
+        and old_factors.shape == (16, 128, 128)
+        and activations.shape == grads_out.shape == (1024, 1024)
+    )
+    chosen = fused_step if fits else body
+    return chosen(
+        activations, grads_out, grad_parts, old_factors, block_owner, weights, momentum
+    )
+
+
 def solution(mesh):
     placed = (
         P(("shards", "tensor", "replica"), None),
@@ -131,7 +553,7 @@
         P(("shards", "replica"), "tensor"),
     )
     return jax.shard_map(
-        body,
+        step,
         mesh=mesh,
         in_specs=placed,
         out_specs=(P(None, "tensor"), P(("shards", "replica"), "tensor"), P("shards", None, None)),

time: 398 us -> 76.8 us (0.19)
  waiting for transfers between devices: 305 us -> 0 us
  Pallas kernels: 0 us -> 65.1 us
  blocking collectives: 40.3 us -> 0 us
  matrix products: 18.2 us -> 0 us
  between operations: 16.6 us -> 0.66 us
  other arithmetic: 5.67 us -> 0 us
    psum x1 -> x0, waiting for transfers between devices: 135 us -> none  [body(): summed = lax.psum(packed, ('shards', 'tensor', 'replica'))]
    reduce_scatter x2 -> x0, waiting for transfers between devices: 109 us -> none  [the longest x1 67.5 us: body(): lax.psum_scatter(precond, ('shards', 'replica'), scatter_dimension=0, til...]
    pallas_call x0 -> x1, Pallas kernels: none -> 65.1 us  [fused_step(): pl.pallas_call(functools.partial(fused_kernel, float(activations.shape[0]...]
    all_gather x2 -> x0, waiting for transfers between devices: 60.8 us -> none  [the longest x1 39.7 us: body(): lax.all_gather(weights_next, ('shards', 'replica'), axis=0, tiled=True)]
    psum x1 -> x0, blocking collectives: 40.3 us -> none  [body(): lax.psum(jnp.sum(total_precond * total_grad), ('shards', 'tensor', 'repli...]
    dot_general x15 -> x0, matrix products: 18.2 us -> none  [the longest x4 3.66 us: newton_inverse(): jnp.einsum('nab,nbc->nac', left_part, approx, precision=exact_mode)]
    unnamed x21 -> x17, local copies, waits for them, and re-layouts: 6.55 us -> 10.5 us
  transfers between devices with their start and end apart: 5 -> 0, of which waited for: 5 -> 0; matrix products, arithmetic and copies ran while one was open for 3% -> 0% of each run, Pallas kernels for 0% -> 0%
where the time goes in v1:
time: 76.8 us; the launch traced here: 76.2 us
  Pallas kernels  65.1 us (85%)
  local copies, waits for them, and re-layouts  10.5 us (14%)
    pallas_call x1, Pallas kernels, fused_step(): pl.pallas_call(functools.partial(fused_kernel, float(activations.shape[0]...  65.1 us
    unnamed x17, local copies, waits for them, and re-layouts  10.5 us

profile of v1, /device:TPU:0, one launch (start us, length us, event | category | flops | bytes accessed | tf_op | source)
XLA Modules:
  0.0 76.2 jit_solution(7393172266608118942)
XLA Ops:
  0.6 0.0 copy-start
  0.6 1.6 %copy-done = bf16[1024,1024]{1,0:T(8,128)(2,1)S(1)} copy-done((bf16[1024,1024]{1,0:T(8,128)(2,1)S(1)}, bf16[1024,1024]{1,0:T(8,128)(2,1)}, u32[]{:S(2)}) %copy-start) | copy-done | bytes 2097176
  2.2 0.0 copy-start.1
  2.2 1.6 %copy-done.1 = bf16[1024,1024]{1,0:T(8,128)(2,1)S(1)} copy-done((bf16[1024,1024]{1,0:T(8,128)(2,1)S(1)}, bf16[1024,1024]{1,0:T(8,128)(2,1)}, u32[]{:S(2)}) %copy-start.1) | copy-done | bytes 2097176
  3.8 0.0 copy-start.2
  3.8 1.2 %copy-done.2 = f32[1,1024,256]{2,1,0:T(8,128)S(1)} copy-done((f32[1,1024,256]{2,1,0:T(8,128)S(1)}, f32[1,1024,256]{2,1,0:T(8,128)}, u32[]{:S(2)}) %copy-start.2) | copy-done | bytes 1048600
  5.0 0.0 copy-start.3
  5.0 1.2 %copy-done.3 = f32[16,128,128]{2,1,0:T(8,128)S(1)} copy-done((f32[16,128,128]{2,1,0:T(8,128)S(1)}, f32[16,128,128]{2,1,0:T(8,128)}, u32[]{:S(2)}) %copy-start.3) | copy-done | bytes 1048600
  6.3 0.0 copy-start.4
  6.3 0.9 %copy-done.4 = f32[128,256]{1,0:T(8,128)S(1)} copy-done((f32[128,256]{1,0:T(8,128)S(1)}, f32[128,256]{1,0:T(8,128)}, u32[]{:S(2)}) %copy-start.4) | copy-done | bytes 131096
  7.2 0.0 copy-start.5
  7.2 0.9 %copy-done.5 = f32[128,256]{1,0:T(8,128)S(1)} copy-done((f32[128,256]{1,0:T(8,128)S(1)}, f32[128,256]{1,0:T(8,128)}, u32[]{:S(2)}) %copy-start.5) | copy-done | bytes 131096
  8.1 0.0 copy-start.6
  8.1 0.7 copy-done.6
  8.7 65.1 %shard_map.94 = (f32[1024,256]{1,0:T(8,128)S(1)}, f32[128,256]{1,0:T(8,128)S(1)}, f32[9,128,128]{2,1,0:T(8,128)S(1)}) custom-call(s32[16]{0:T(128)S(1)} %copy-done.6, bf16[1024,1024]{1,0:T(8,128)(2,1)S(1)} %copy-done, bf16[1024,1024]{1,0:T(8,128)(2,1)S(1)} %copy-done.1, f32[1,1024,256]{2,1,0:T(8,128)S(1)} %copy-done.2, f32[16,128,128]{2,1,0:T(8,128)S(1)} %copy-done.3, ...), custom_call_target="tpu_custom_call" | custom-call | flops 1200000000 | bytes 10000000 | tf_op jit(solution)/shard_map/pallas_call | solution.py:479
  73.8 1.0 %copy.13 = f32[1024,256]{1,0:T(8,128)} copy(f32[1024,256]{1,0:T(8,128)S(1)} %get-tuple-element.6) | data formatting | bytes 2097152
  74.8 0.7 copy.14
  75.4 0.8 %copy.15 = f32[9,128,128]{2,1,0:T(8,128)} copy(f32[9,128,128]{2,1,0:T(8,128)S(1)} %get-tuple-element.8) | data formatting | bytes 1179648
Async XLA Ops:
  0.6 1.6 %copy-start = (bf16[1024,1024]{1,0:T(8,128)(2,1)S(1)}, bf16[1024,1024]{1,0:T(8,128)(2,1)}, u32[]{:S(2)}) copy-start(bf16[1024,1024]{1,0:T(8,128)(2,1)} %act_ref.1) | copy-start | bytes 6291460
  2.2 1.6 %copy-start.1 = (bf16[1024,1024]{1,0:T(8,128)(2,1)S(1)}, bf16[1024,1024]{1,0:T(8,128)(2,1)}, u32[]{:S(2)}) copy-start(bf16[1024,1024]{1,0:T(8,128)(2,1)} %gout_ref.1) | copy-start | bytes 6291460
  3.8 1.2 %copy-start.2 = (f32[1,1024,256]{2,1,0:T(8,128)S(1)}, f32[1,1024,256]{2,1,0:T(8,128)}, u32[]{:S(2)}) copy-start(f32[1,1024,256]{2,1,0:T(8,128)} %grad_ref.1) | copy-start | bytes 3145732
  5.0 1.2 %copy-start.3 = (f32[16,128,128]{2,1,0:T(8,128)S(1)}, f32[16,128,128]{2,1,0:T(8,128)}, u32[]{:S(2)}) copy-start(f32[16,128,128]{2,1,0:T(8,128)} %old_ref.1) | copy-start | bytes 3145732
  6.3 0.9 %copy-start.4 = (f32[128,256]{1,0:T(8,128)S(1)}, f32[128,256]{1,0:T(8,128)}, u32[]{:S(2)}) copy-start(f32[128,256]{1,0:T(8,128)} %weights_ref.1) | copy-start | bytes 393220
  7.2 0.9 %copy-start.5 = (f32[128,256]{1,0:T(8,128)S(1)}, f32[128,256]{1,0:T(8,128)}, u32[]{:S(2)}) copy-start(f32[128,256]{1,0:T(8,128)} %momentum_ref.1) | copy-start | bytes 393220
  8.1 0.7 copy-start.6

commit v2 on v1

--- a/solution.py
+++ b/solution.py
@@ -144,8 +144,23 @@
     return first, second
 
 
+def split_halves(a):
+    high = a.astype(jnp.bfloat16)
+    return high, (a - high.astype(jnp.float32)).astype(jnp.bfloat16)
+
+
 def dot_exact(a, b):
-    return jnp.dot(a, b, precision=exact_mode, preferred_element_type=jnp.float32)
+    a_high, a_low = split_halves(a)
+    b_high, b_low = split_halves(b)
+    dot = functools.partial(jnp.dot, preferred_element_type=jnp.float32)
+    return dot(a_high, b_high) + (dot(a_high, b_low) + dot(a_low, b_high))
+
+
+def ordered_sum(ref, count):
+    terms = [ref[k] for k in range(count)]
+    while len(terms) > 1:
+        terms = [terms[k] + terms[k + 1] for k in range(0, len(terms), 2)]
+    return terms[0]
 
 
 def fused_kernel(
@@ -162,24 +177,26 @@
     factors_out,
     act_v,
     gout_v,
+    old_v,
+    weights_v,
+    momentum_v,
     packed_v,
     core_in,
     y_in,
-    z_out,
-    z_in,
-    x_out,
-    x_in,
+    xz_out,
+    xz_in,
     full_v,
     diag_out,
     diag_in,
-    diag_z,
+    diag_xz,
     grad_own,
     grad_x,
     grad_z,
     sum_out,
     sum_xz,
     sum_tensor,
-    new_weights,
+    base_all,
+    precond_all,
     mixed_v,
     local_sem,
     sends,
@@ -193,51 +210,50 @@
     n = 128
     half = 512
     quarter = 256
+    place = s * 4 + r
     x_peer = (1 - s, t, r)
     y_peer = (s, 2 * (1 - y) + c, r)
     c_peer = (s, 2 * y + 1 - c, r)
     yc_peer = (s, 2 * (1 - y) + 1 - c, r)
     z_ranks = [(r + d) % 4 for d in (1, 2, 3)]
     z_peers = [(s, t, q) for q in z_ranks]
-    xz_peers = [(1 - s, t, q) for q in z_ranks]
+    xz_peers = z_peers + [(1 - s, t, q) for q in z_ranks] + [x_peer]
+    xz_places = [s * 4 + q for q in z_ranks] + [(1 - s) * 4 + q for q in z_ranks]
+    xz_places = xz_places + [(1 - s) * 4 + r]
+    used_sems = [0]
 
     def part(ref, start, size):
         return ref.at[pl.ds(pl.multiple_of(start, 8), size)]
 
-    loads = []
-    for k, core in enumerate((1 - c, c)):
-        columns = pl.ds(pl.multiple_of(core * half, half), half)
-        for src, dst in ((act_ref, act_v), (gout_ref, gout_v)):
-            copy = pltpu.make_async_copy(
-                src.at[:, columns], dst.at[:, columns], local_sem.at[len(loads)]
-            )
-            copy.start()
-            loads.append(copy)
-    own_load = pltpu.make_async_copy(
-        grad_ref.at[0, pl.ds(pl.multiple_of(s * half, half), half)], grad_own, local_sem.at[4]
-    )
-    own_load.start()
+    def send(src, dst, device):
+        copy = remote(src, dst, sends, recvs, used_sems[0], device)
+        used_sems[0] += 1
+        copy.start()
+        return copy
+
+    def load(src, dst, index):
+        copy = pltpu.make_async_copy(src, dst, local_sem.at[index])
+        copy.start()
+        return copy
 
     barrier = pltpu.get_barrier_semaphore()
-    peers = [x_peer, y_peer, c_peer, yc_peer] + z_peers + xz_peers
+    peers = xz_peers + [y_peer, c_peer, yc_peer]
     for peer in peers:
         pl.semaphore_signal(barrier, inc=1, device_id=peer, device_id_type=MESH)
-    pl.semaphore_wait(barrier, len(peers))
-
-    count = 0
-    grad_x_copies = []
-    for k in range(4):
-        copy = remote(
-            grad_ref.at[0, pl.ds(pl.multiple_of((1 - s) * half + k * n, n), n)],
-            grad_x.at[k],
-            sends,
-            recvs,
-            count,
-            x_peer,
-        )
-        count += 1
-        copy.start()
-        grad_x_copies.append(copy)
+
+    groups = ((1 - y, 1 - c), (y, 1 - c), (1 - y, c), (y, c))
+    starts = [pl.multiple_of(side * half + core * quarter, quarter) for side, core in groups]
+    loads = []
+    for k, start in enumerate(starts):
+        columns = pl.ds(start, quarter)
+        loads.append(load(act_ref.at[:, columns], act_v.at[:, columns], 2 * k))
+        loads.append(load(gout_ref.at[:, columns], gout_v.at[:, columns], 2 * k + 1))
+    weights_load = load(weights_ref, weights_v, 8)
+    momentum_load = load(momentum_ref, momentum_v, 9)
+    own_load = load(
+        grad_ref.at[0, pl.ds(pl.multiple_of(s * half, half), half)], grad_own, 10
+    )
+    old_load = load(old_ref, old_v, 11)
 
     rows = lax.broadcasted_iota(jnp.int32, (n, n), 0)
     cols = lax.broadcasted_iota(jnp.int32, (n, n), 1)
@@ -248,15 +264,12 @@
 
     diag = jnp.zeros((8, n), jnp.float32)
     core_copies = []
-    y_copy = None
-    for j, (core, side) in enumerate(((1 - c, 1 - y), (1 - c, y), (c, 1 - y), (c, y))):
-        if j % 2 == 0:
-            loads[j].wait()
-            loads[j + 1].wait()
-        start = pl.multiple_of(core * half + side * quarter, quarter)
-        columns = pl.ds(start, quarter)
-        a = act_v[:, columns]
-        g = gout_v[:, columns]
+    for j, (side, core) in enumerate(groups):
+        loads[2 * j].wait()
+        loads[2 * j + 1].wait()
+        start = starts[j]
+        a = act_v[:, pl.ds(start, quarter)]
+        g = gout_v[:, pl.ds(start, quarter)]
         across = (((0,), (0,)), ((), ()))
         left = lax.dot_general(a, a, across, preferred_element_type=jnp.float32)
         right = lax.dot_general(g, g, across, preferred_element_type=jnp.float32)
@@ -265,181 +278,194 @@
             second = right[span, span]
             packed_v[pl.ds(start + k * n, n), :] = jnp.where(lower, second, left[span, span])
             row = jnp.sum(jnp.where(on_diagonal, second, 0.0), axis=0, keepdims=True)
-            diag = jnp.where(pair_rows == core * 4 + side * 2 + k, row, diag)
+            diag = jnp.where(pair_rows == side * 4 + core * 2 + k, row, diag)
+        if j == 0:
+            pl.semaphore_wait(barrier, len(peers))
         if j < 2:
-            copy = remote(
-                part(packed_v, start, quarter), core_in.at[j], sends, recvs, count, c_peer
-            )
-            count += 1
-            copy.start()
-            core_copies.append(copy)
+            core_copies.append(send(part(packed_v, start, quarter), core_in.at[j], c_peer))
+        if j == 0:
+            grad_x_copies = [
+                send(
+                    grad_ref.at[0, pl.ds(pl.multiple_of((1 - s) * half + k * n, n), n)],
+                    grad_x.at[k],
+                    x_peer,
+                )
+                for k in range(4)
+            ]
+        elif j == 1:
+            weights_load.wait()
+            momentum_load.wait()
+            own_rows = pl.ds(pl.multiple_of(place * n, n), n)
+            base_all[own_rows, :] = weights_v[...] - (step_rate * momentum_rate) * momentum_v[...]
+            base_own = part(base_all, place * n, n)
+            base_copies = [send(base_own, base_own, peer) for peer in z_peers]
         elif j == 2:
             core_copies[0].wait()
             packed_v[pl.ds(start, quarter), :] += core_in[0]
-            y_copy = remote(part(packed_v, start, quarter), y_in, sends, recvs, count, y_peer)
-            count += 1
-            y_copy.start()
+            y_copy = send(part(packed_v, start, quarter), y_in, y_peer)
     diag_out[0] = diag
-    copy = remote(diag_out.at[0], diag_in.at[0], sends, recvs, count, c_peer)
-    count += 1
-    copy.start()
+    copy = send(diag_out.at[0], diag_in.at[0], c_peer)
     core_copies[1].wait()
+    mine = packed_v[pl.ds(starts[3], quarter), :] + core_in[1]
     copy.wait()
     diag = diag + diag_in[0]
     diag_out[1] = diag
-    diag_copy = remote(diag_out.at[1], diag_in.at[1], sends, recvs, count, y_peer)
-    count += 1
-    diag_copy.start()
-    start = pl.multiple_of(c * half + y * quarter, quarter)
-    mine = packed_v[pl.ds(start, quarter), :] + core_in[1]
+    diag_copy = send(diag_out.at[1], diag_in.at[1], y_peer)
     y_copy.wait()
-    z_out[...] = (mine + y_in[...]).reshape(4, 64, n)
-    z_copies = []
-    for d in range(3):
-        copy = remote(z_out.at[z_ranks[d]], z_in.at[r], sends, recvs, count, z_peers[d])
-        count += 1
-        copy.start()
-        z_copies.append(copy)
+    xz_out[...] = (mine + y_in[...]).reshape(8, 32, n)
+    copies = [
+        send(xz_out.at[q], xz_in.at[place], peer) for q, peer in zip(xz_places, xz_peers)
+    ]
     diag_copy.wait()
     diag = diag + diag_in[1]
     diag_out[2] = diag
-    for d in range(3):
-        copy = remote(diag_out.at[2], diag_z.at[r], sends, recvs, count, z_peers[d])
-        count += 1
-        copy.start()
-        z_copies.append(copy)
-    z_in[r] = z_out[r]
-    diag_z[r] = diag
-    for copy in z_copies:
-        copy.wait()
-    x_out[...] = (z_in[0] + z_in[1]) + (z_in[2] + z_in[3])
-    x_copy = remote(part(x_out, (1 - s) * 32, 32), x_in, sends, recvs, count, x_peer)
-    count += 1
-    x_copy.start()
-    diag = (diag_z[0] + diag_z[1]) + (diag_z[2] + diag_z[3])
-    diag_out[3] = diag
-    diag_copy = remote(diag_out.at[3], diag_in.at[2], sends, recvs, count, x_peer)
-    count += 1
-    diag_copy.start()
-    x_copy.wait()
-    z_base = c * half + y * quarter + r * 64
-    start = pl.multiple_of(z_base + s * 32, 32)
-    full_v[pl.ds(start, 32), :] = x_out[pl.ds(pl.multiple_of(s * 32, 32), 32), :] + x_in[...]
+    diag_copies = [send(diag_out.at[2], diag_xz.at[place], peer) for peer in xz_peers]
+    xz_in[place] = xz_out[place]
+    diag_xz[place] = diag
+    for copy in copies:
+        copy.wait()
+    start = pl.multiple_of(starts[3] + place * 32, 32)
+    full_v[pl.ds(start, 32), :] = ordered_sum(xz_in, 8)
     region = part(full_v, start, 32)
-    copy = remote(region, region, sends, recvs, count, x_peer)
-    count += 1
-    copy.start()
-    diag_copy.wait()
-    diag = diag + diag_in[2]
-    diag_out[4] = diag
-    copy.wait()
-    z_copies = []
-    region = part(full_v, z_base, 64)
-    for d in range(3):
-        copy = remote(region, region, sends, recvs, count, z_peers[d])
-        count += 1
-        copy.start()
-        z_copies.append(copy)
+    copies = [send(region, region, peer) for peer in xz_peers]
+    for copy in diag_copies:
+        copy.wait()
+    diag_out[3] = ordered_sum(diag_xz, 8)
     own_load.wait()
-    for copy in z_copies:
-        copy.wait()
-    region = part(full_v, c * half + y * quarter, quarter)
-    y_copy = remote(region, region, sends, recvs, count, y_peer)
-    count += 1
-    y_copy.start()
     for k in range(4):
         grad_x_copies[k].wait()
         grad_x[k] = grad_x[k] + grad_own[pl.ds(k * n, n), :]
-    grad_copies = []
-    for d in range(3):
-        copy = remote(grad_x.at[z_ranks[d]], grad_z.at[r], sends, recvs, count, z_peers[d])
-        count += 1
-        copy.start()
-        grad_copies.append(copy)
+    for copy in copies:
+        copy.wait()
+    region = part(full_v, starts[3], quarter)
+    y_copy = send(region, region, y_peer)
+    core_copies = [send(region, region, c_peer)]
+    grad_copies = [
+        send(grad_x.at[q], grad_z.at[r], peer) for q, peer in zip(z_ranks, z_peers)
+    ]
     grad_z[r] = grad_x[r]
-    y_copy.wait()
-    region = part(full_v, c * half, half)
-    copy = remote(region, region, sends, recvs, count, c_peer)
-    count += 1
-    copy.start()
-    copy.wait()
+    for copy in base_copies:
+        copy.wait()
+    region = part(base_all, s * half, half)
+    base_copy = send(region, region, x_peer)
 
     def blend(pair):
         first, second = unpack_pair(
             full_v[pl.ds(pl.multiple_of(pair * n, n), n), :],
-            diag_out[4, pl.ds(pair, 1), :],
+            diag_out[3, pl.ds(pair, 1), :],
             lower,
             on_diagonal,
         )
         return (
-            decay_rate * old_ref[pair] + (1.0 - decay_rate) * (first / sample_total),
-            decay_rate * old_ref[8 + pair] + (1.0 - decay_rate) * (second / sample_total),
+            decay_rate * old_v[pair] + (1.0 - decay_rate) * (first / sample_total),
+            decay_rate * old_v[8 + pair] + (1.0 - decay_rate) * (second / sample_total),
         )
 
-    mixed = [blend(s * 4 + r)[0], blend(2 * t)[1], blend(2 * t + 1)[1]]
-    scales, rests = [], []
-    for block in mixed:
-        trace = jnp.sum(jnp.where(on_diagonal, block, 0.0), keepdims=True)
-        damped = block + (damping * trace / n + damp_shift) * identity
-        bound = jnp.max(
-            jnp.sum(jnp.abs(damped), axis=1, keepdims=True), axis=0, keepdims=True
-        )
-        scales.append(1.0 / bound)
-        rests.append(identity - damped / bound)
-    inverses = [identity + rest for rest in rests]
-    for _ in range(NS_STEPS - 1):
-        rests = [dot_exact(rest, rest) for rest in rests]
-        inverses = [inv + dot_exact(inv, rest) for inv, rest in zip(inverses, rests)]
-    inverses = [inv * scale for inv, scale in zip(inverses, scales)]
+    def invert(blocks):
+        scales, rests = [], []
+        for block in blocks:
+            trace = jnp.sum(jnp.where(on_diagonal, block, 0.0), keepdims=True)
+            damped = block + (damping * trace / n + damp_shift) * identity
+            bound = jnp.max(
+                jnp.sum(jnp.abs(damped), axis=1, keepdims=True), axis=0, keepdims=True
+            )
+            scales.append(1.0 / bound)
+            rests.append(identity - damped / bound)
+        inverses = [identity + rest for rest in rests]
+        for _ in range(NS_STEPS - 1):
+            rests = [dot_exact(rest, rest) for rest in rests]
+            inverses = [inv + dot_exact(inv, rest) for inv, rest in zip(inverses, rests)]
+        return [inv * scale for inv, scale in zip(inverses, scales)]
+
+    old_load.wait()
+    right_inverses = invert([blend(2 * t)[1], blend(2 * t + 1)[1]])
+    y_copy.wait()
+    region = part(full_v, starts[2], quarter)
+    core_copies.append(send(region, region, c_peer))
+    for copy in core_copies:
+        copy.wait()
+    left_inverse = invert([blend(place)[0]])[0]
 
     for copy in grad_copies:
         copy.wait()
     gradient = (grad_z[0] + grad_z[1]) + (grad_z[2] + grad_z[3])
-    left = dot_exact(inverses[0], gradient)
+    left = dot_exact(left_inverse, gradient)
     precond = jnp.concatenate(
-        [dot_exact(left[:, :n], inverses[1]), dot_exact(left[:, n:], inverses[2])], axis=1
+        [dot_exact(left[:, k * n : (k + 1) * n], right_inverses[k]) for k in range(2)], axis=1
     )
     products = precond * gradient
     products = products[:, :n] + products[:, n:]
     tile = jnp.sum(products.reshape(16, 8, n), axis=0)
 
-    place = s * 4 + r
     sum_out[0] = tile
-    sum_copies = []
-    for peer in [x_peer] + z_peers + xz_peers:
-        copy = remote(sum_out.at[0], sum_xz.at[place], sends, recvs, count, peer)
-        count += 1
-        copy.start()
-        sum_copies.append(copy)
+    sum_copies = [send(sum_out.at[0], sum_xz.at[place], peer) for peer in xz_peers]
+    precond_all[pl.ds(pl.multiple_of(place * n, n), n), :] = precond
+    own = part(precond_all, place * n, n)
+    x_copies = [send(own, own, x_peer)]
+
+    first_sem = used_sems[0]
+    used_sems[0] += 14
+
+    def passing(hop, way, peer, hand_on):
+        origin = r - hop if way == 0 else r + hop
+        region = part(precond_all, (s * 4 + origin) * n, n)
+        index = first_sem + 6 * hand_on + 2 * hop + way
+        return remote(region, region, sends, recvs, index, peer)
+
+    ways = ((s, t, r + 1), (s, t, r - 1))
+
+    def sends_on(hop, way):
+        return (r >= hop) & (r < 3) if way == 0 else (r <= 3 - hop) & (r > 0)
+
+    def gets(hop, way):
+        return r >= hop + 1 if way == 0 else r <= 2 - hop
+
+    def start_hop(hop):
+        for way in range(2):
+
+            @pl.when(sends_on(hop, way))
+            def _():
+                passing(hop, way, ways[way], 0).start()
+
+    def arrived(hop):
+        for way in range(2):
+
+            @pl.when(gets(hop, way))
+            def _():
+                back = ways[1 - way]
+                origin = r - hop - 1 if way == 0 else r + hop + 1
+                region = part(precond_all, (s * 4 + origin) * n, n)
+                index = first_sem + 2 * hop + way
+                remote(region, region, sends, recvs, index, back).wait_recv()
+
+    def hand_on(hop):
+        for way in range(2):
+
+            @pl.when(gets(hop, way))
+            def _():
+                passing(hop + 1, way, x_peer, 1).start()
+
+    start_hop(0)
     sum_xz[place] = tile
     for copy in sum_copies:
         copy.wait()
-    tile = jnp.sum(sum_xz[...], axis=0)
+    tile = ordered_sum(sum_xz, 8)
     sum_out[1] = tile
-    sum_copies = []
-    for peer in (c_peer, y_peer, yc_peer):
-        copy = remote(sum_out.at[1], sum_tensor.at[t], sends, recvs, count, peer)
-        count += 1
-        copy.start()
-        sum_copies.append(copy)
+    sum_copies = [
+        send(sum_out.at[1], sum_tensor.at[t], peer) for peer in (c_peer, y_peer, yc_peer)
+    ]
     sum_tensor[t] = tile
+    arrived(0)
+    start_hop(1)
+    hand_on(0)
     for copy in sum_copies:
         copy.wait()
-    alignment = jnp.sum(jnp.sum(sum_tensor[...], axis=0), keepdims=True)
+    alignment = jnp.sum(ordered_sum(sum_tensor, 4), keepdims=True)
     clip_scale = jnp.minimum(1.0, clip_norm / jnp.sqrt(alignment))
-    momentum_next = momentum_rate * momentum_ref[...] + clip_scale * precond
-    momentum_out[...] = momentum_next
-    new_weights[...] = weights_ref[...] - step_rate * momentum_next
-
-    target = part(weights_out, place * n, n)
-    own_store = pltpu.make_async_copy(new_weights, target, local_sem.at[5])
-    own_store.start()
-    gather = []
-    for peer in z_peers + [x_peer]:
-        copy = remote(new_weights, target, sends, recvs, count, peer)
-        count += 1
-        copy.start()
-        gather.append(copy)
+    momentum_out[...] = momentum_rate * momentum_v[...] + clip_scale * precond
+    arrived(1)
+    start_hop(2)
+    hand_on(1)
 
     for pair in range(8):
         mixed_v[pair], mixed_v[8 + pair] = blend(pair)
@@ -455,17 +481,23 @@
     for k in range(len(chosen)):
         factors_out[k] = mixed_v[chosen[k]]
 
-    for d in range(3):
-        gather[d].wait()
-        origin = s * 4 + (r + 3 - d) % 4
-        region = part(weights_out, origin * n, n)
-        copy = remote(region, region, sends, recvs, count, x_peer)
-        count += 1
-        copy.start()
-        gather.append(copy)
-    for copy in gather[3:]:
-        copy.wait()
-    own_store.wait()
+    arrived(2)
+    hand_on(2)
+    base_copy.wait()
+    for copy in x_copies:
+        copy.wait()
+    for hop in range(3):
+        for way in range(2):
+
+            @pl.when(sends_on(hop, way))
+            def _():
+                passing(hop, way, ways[way], 0).wait_send()
+
+            @pl.when(gets(hop, way))
+            def _():
+                passing(hop + 1, way, x_peer, 1).wait()
+
+    weights_out[...] = base_all[...] - (step_rate * clip_scale) * precond_all[...]
 
 
 def fused_step(activations, grads_out, grad_parts, old_factors, block_owner, weights, momentum):
@@ -488,39 +520,41 @@
             anywhere,
             anywhere,
             anywhere,
-            vmem,
-            vmem,
-            vmem,
+            anywhere,
+            anywhere,
+            anywhere,
         ],
-        out_specs=(anywhere, vmem, vmem),
+        out_specs=(vmem, vmem, vmem),
         scratch_shapes=[
             pltpu.VMEM(activations.shape, activations.dtype),
             pltpu.VMEM(grads_out.shape, grads_out.dtype),
+            pltpu.VMEM(old_factors.shape, f32),
+            pltpu.VMEM(weights.shape, f32),
+            pltpu.VMEM(momentum.shape, f32),
             pltpu.VMEM((1024, n), f32),
             pltpu.VMEM((2, 256, n), f32),
             pltpu.VMEM((256, n), f32),
-            pltpu.VMEM((4, 64, n), f32),
-            pltpu.VMEM((4, 64, n), f32),
-            pltpu.VMEM((64, n), f32),
-            pltpu.VMEM((32, n), f32),
+            pltpu.VMEM((8, 32, n), f32),
+            pltpu.VMEM((8, 32, n), f32),
             pltpu.VMEM((1024, n), f32),
-            pltpu.VMEM((5, 8, n), f32),
-            pltpu.VMEM((3, 8, n), f32),
             pltpu.VMEM((4, 8, n), f32),
+            pltpu.VMEM((2, 8, n), f32),
+            pltpu.VMEM((8, 8, n), f32),
             pltpu.VMEM((512, 256), f32),
             pltpu.VMEM((4, n, 256), f32),
             pltpu.VMEM((4, n, 256), f32),
             pltpu.VMEM((2, 8, n), f32),
             pltpu.VMEM((8, 8, n), f32),
             pltpu.VMEM((4, 8, n), f32),
-            pltpu.VMEM((n, 256), f32),
+            pltpu.VMEM((1024, 256), f32),
+            pltpu.VMEM((1024, 256), f32),
             pltpu.VMEM((17, n, n), f32),
-            pltpu.SemaphoreType.DMA((6,)),
-            pltpu.SemaphoreType.DMA((48,)),
-            pltpu.SemaphoreType.DMA((48,)),
+            pltpu.SemaphoreType.DMA((12,)),
+            pltpu.SemaphoreType.DMA((72,)),
+            pltpu.SemaphoreType.DMA((72,)),
         ],
         compiler_params=pltpu.CompilerParams(
-            collective_id=0, has_side_effects=True, vmem_limit_bytes=40 * 1024 * 1024
+            collective_id=0, has_side_effects=True, vmem_limit_bytes=60 * 1024 * 1024
         ),
         cost_estimate=pl.CostEstimate(
             flops=1_200_000_000, bytes_accessed=10_000_000, transcendentals=0

time: 76.8 us -> 63.7 us (0.83)
  local copies, waits for them, and re-layouts: 10.5 us -> 3.81 us
  Pallas kernels: 65.1 us -> 59.1 us
    unnamed x17 -> x7, local copies, waits for them, and re-layouts: 10.5 us -> 3.81 us
    pallas_call x1, Pallas kernels: 65.1 us -> 59.1 us  [fused_step(): pl.pallas_call(functools.partial(fused_kernel, float(activations.shape[0]...]
where the time goes in v2:
time: 63.7 us; the launch traced here: 63.5 us
  Pallas kernels  59.1 us (93%)
  local copies, waits for them, and re-layouts  3.81 us (6%)
  between operations  0.66 us (1%)
    pallas_call x1, Pallas kernels, fused_step(): pl.pallas_call(functools.partial(fused_kernel, float(activations.shape[0]...  59.1 us
    unnamed x7, local copies, waits for them, and re-layouts  3.81 us

profile of v2, /device:TPU:0, one launch (start us, length us, event | category | flops | bytes accessed | tf_op | source)
XLA Modules:
  0.0 63.5 jit_solution(4180238104901560598)
XLA Ops:
  0.6 59.1 %shard_map.94 = (f32[1024,256]{1,0:T(8,128)}, f32[128,256]{1,0:T(8,128)}, f32[9,128,128]{2,1,0:T(8,128)}) custom-call(s32[16]{0:T(128)} %owner_ref.1, bf16[1024,1024]{1,0:T(8,128)(2,1)} %act_ref.1, bf16[1024,1024]{1,0:T(8,128)(2,1)} %gout_ref.1, f32[1,1024,256]{2,1,0:T(8,128)} %grad_ref.1, f32[16,128,128]{2,1,0:T(8,128)} %old_ref.1, f32[128,256]{1,0:T(8,128)} %weights_ref.1, ...), custom_call_target="tpu_custom_call" | custom-call | flops 1200000000 | bytes 10000000 | tf_op jit(solution)/shard_map/pallas_call | solution.py:511
  59.7 0.0 copy-start.1
  59.7 0.0 copy-start
  59.7 2.3 %copy.13 = f32[1024,256]{1,0:T(8,128)} copy(f32[1024,256]{1,0:T(8,128)} %get-tuple-element.6) | data formatting | bytes 2097152
  62.0 0.0 copy-done.1
  62.0 0.7 %copy.14 = f32[128,256]{1,0:T(8,128)} copy(f32[128,256]{1,0:T(8,128)S(1)} %copy-done.1) | data formatting | bytes 262144
  62.7 0.0 copy-done
  62.7 0.8 %copy.15 = f32[9,128,128]{2,1,0:T(8,128)} copy(f32[9,128,128]{2,1,0:T(8,128)S(1)} %copy-done) | data formatting | bytes 1179648
Async XLA Ops:
  59.7 2.4 %copy-start.1 = (f32[128,256]{1,0:T(8,128)S(1)}, f32[128,256]{1,0:T(8,128)}, u32[]{:S(2)}) copy-start(f32[128,256]{1,0:T(8,128)} %get-tuple-element.7) | copy-start | bytes 393220
  59.7 3.0 %copy-start = (f32[9,128,128]{2,1,0:T(8,128)S(1)}, f32[9,128,128]{2,1,0:T(8,128)}, u32[]{:S(2)}) copy-start(f32[9,128,128]{2,1,0:T(8,128)} %get-tuple-element.8) | copy-start | bytes 1769476

commit v3 on v2

--- a/solution.py
+++ b/solution.py
@@ -186,6 +186,7 @@
     xz_out,
     xz_in,
     full_v,
+    left_pair,
     diag_out,
     diag_in,
     diag_xz,
@@ -322,6 +323,14 @@
     diag_copies = [send(diag_out.at[2], diag_xz.at[place], peer) for peer in xz_peers]
     xz_in[place] = xz_out[place]
     diag_xz[place] = diag
+    own_load.wait()
+    for k in range(4):
+        grad_x_copies[k].wait()
+        grad_x[k] = grad_x[k] + grad_own[pl.ds(k * n, n), :]
+    grad_copies = [
+        send(grad_x.at[q], grad_z.at[r], peer) for q, peer in zip(z_ranks, z_peers)
+    ]
+    grad_z[r] = grad_x[r]
     for copy in copies:
         copy.wait()
     start = pl.multiple_of(starts[3] + place * 32, 32)
@@ -331,27 +340,43 @@
     for copy in diag_copies:
         copy.wait()
     diag_out[3] = ordered_sum(diag_xz, 8)
-    own_load.wait()
-    for k in range(4):
-        grad_x_copies[k].wait()
-        grad_x[k] = grad_x[k] + grad_own[pl.ds(k * n, n), :]
     for copy in copies:
         copy.wait()
+
+    holder = (s == y) & (r // 2 == c)
+    pair_sem = used_sems[0]
+    used_sems[0] += 3
+    pair_copies = [
+        pltpu.make_async_remote_copy(
+            src_ref=part(full_v, place * n, n),
+            dst_ref=left_pair,
+            send_sem=sends.at[pair_sem + k],
+            recv_sem=recvs.at[pair_sem],
+            device_id=peer,
+            device_id_type=MESH,
+        )
+        for k, peer in enumerate((yc_peer, y_peer, c_peer))
+    ]
+
+    @pl.when(holder)
+    def _():
+        for copy in pair_copies:
+            copy.start()
+        left_pair[...] = full_v[pl.ds(pl.multiple_of(place * n, n), n), :]
+
     region = part(full_v, starts[3], quarter)
     y_copy = send(region, region, y_peer)
     core_copies = [send(region, region, c_peer)]
-    grad_copies = [
-        send(grad_x.at[q], grad_z.at[r], peer) for q, peer in zip(z_ranks, z_peers)
-    ]
-    grad_z[r] = grad_x[r]
     for copy in base_copies:
         copy.wait()
     region = part(base_all, s * half, half)
     base_copy = send(region, region, x_peer)
 
-    def blend(pair):
+    def blend(pair, packed=None):
+        if packed is None:
+            packed = full_v[pl.ds(pl.multiple_of(pair * n, n), n), :]
         first, second = unpack_pair(
-            full_v[pl.ds(pl.multiple_of(pair * n, n), n), :],
+            packed,
             diag_out[3, pl.ds(pair, 1), :],
             lower,
             on_diagonal,
@@ -379,12 +404,15 @@
 
     old_load.wait()
     right_inverses = invert([blend(2 * t)[1], blend(2 * t + 1)[1]])
+
+    @pl.when(jnp.logical_not(holder))
+    def _():
+        pair_copies[0].wait_recv()
+
+    left_inverse = invert([blend(place, left_pair[...])[0]])[0]
     y_copy.wait()
     region = part(full_v, starts[2], quarter)
     core_copies.append(send(region, region, c_peer))
-    for copy in core_copies:
-        copy.wait()
-    left_inverse = invert([blend(place)[0]])[0]
 
     for copy in grad_copies:
         copy.wait()
@@ -466,6 +494,14 @@
     arrived(1)
     start_hop(2)
     hand_on(1)
+
+    for copy in core_copies:
+        copy.wait()
+
+    @pl.when(holder)
+    def _():
+        for copy in pair_copies:
+            copy.wait_send()
 
     for pair in range(8):
         mixed_v[pair], mixed_v[8 + pair] = blend(pair)
@@ -500,6 +536,23 @@
     weights_out[...] = base_all[...] - (step_rate * clip_scale) * precond_all[...]
 
 
+def copy_out_kernel(weights, momentum, factors, weights_out, momentum_out, factors_out, sems):
+    copies = []
+    for src, dst, parts in (
+        (weights, weights_out, 4),
+        (factors, factors_out, 3),
+        (momentum, momentum_out, 1),
+    ):
+        size = src.shape[0] // parts
+        for k in range(parts):
+            span = pl.ds(k * size, size)
+            copy = pltpu.make_async_copy(src.at[span], dst.at[span], sems.at[len(copies)])
+            copy.start()
+            copies.append(copy)
+    for copy in copies:
+        copy.wait()
+
+
 def fused_step(activations, grads_out, grad_parts, old_factors, block_owner, weights, momentum):
     n = old_factors.shape[1]
     shards = lax.axis_size("shards")
@@ -508,7 +561,7 @@
     f32 = jnp.float32
     anywhere = pl.BlockSpec(memory_space=pl.ANY)
     vmem = pl.BlockSpec(memory_space=pltpu.VMEM)
-    return pl.pallas_call(
+    results = pl.pallas_call(
         functools.partial(fused_kernel, float(activations.shape[0] * devices)),
         out_shape=(
             jax.ShapeDtypeStruct(grad_parts.shape[1:], f32),
@@ -537,6 +590,7 @@
             pltpu.VMEM((8, 32, n), f32),
             pltpu.VMEM((8, 32, n), f32),
             pltpu.VMEM((1024, n), f32),
+            pltpu.VMEM((n, n), f32),
             pltpu.VMEM((4, 8, n), f32),
             pltpu.VMEM((2, 8, n), f32),
             pltpu.VMEM((8, 8, n), f32),
@@ -560,6 +614,14 @@
             flops=1_200_000_000, bytes_accessed=10_000_000, transcendentals=0
         ),
     )(block_owner, activations, grads_out, grad_parts, old_factors, weights, momentum)
+    return pl.pallas_call(
+        copy_out_kernel,
+        out_shape=tuple(jax.ShapeDtypeStruct(a.shape, a.dtype) for a in results),
+        in_specs=[anywhere] * 3,
+        out_specs=(anywhere,) * 3,
+        scratch_shapes=[pltpu.SemaphoreType.DMA((8,))],
+        cost_estimate=pl.CostEstimate(flops=0, bytes_accessed=3_500_000, transcendentals=0),
+    )(*results)
 
 
 def step(activations, grads_out, grad_parts, old_factors, block_owner, weights, momentum):

time: 63.7 us -> 122 us (1.92)
  Pallas kernels: 59.1 us -> 121 us
  local copies, waits for them, and re-layouts: 3.81 us -> 0 us
    pallas_call x0 -> x1, Pallas kernels: none -> 54.8 us  [fused_step(): pl.pallas_call(copy_out_kernel, out_shape=tuple((jax.ShapeDtypeStruct(a.s...]
    pallas_call x1, Pallas kernels: 59.1 us -> 66 us  [fused_step(): pl.pallas_call(functools.partial(fused_kernel, float(activations.shape[0]...]
    unnamed x7 -> x0, local copies, waits for them, and re-layouts: 3.81 us -> none
where the time goes in v3:
time: 122 us; the launch traced here: 121 us
  Pallas kernels  121 us (99%)
    pallas_call x1, Pallas kernels, fused_step(): pl.pallas_call(functools.partial(fused_kernel, float(activations.shape[0]...  66 us
    pallas_call x1, Pallas kernels, fused_step(): pl.pallas_call(copy_out_kernel, out_shape=tuple((jax.ShapeDtypeStruct(a.s...  54.8 us

profile of v3, /device:TPU:0, one launch (start us, length us, event | category | flops | bytes accessed | tf_op | source)
XLA Modules:
  0.0 121.5 jit_solution(8729889933341379468)
XLA Ops:
  0.6 66.0 %shard_map.94 = (f32[1024,256]{1,0:T(8,128)}, f32[128,256]{1,0:T(8,128)}, f32[9,128,128]{2,1,0:T(8,128)}) custom-call(s32[16]{0:T(128)} %owner_ref.1, bf16[1024,1024]{1,0:T(8,128)(2,1)} %act_ref.1, bf16[1024,1024]{1,0:T(8,128)(2,1)} %gout_ref.1, f32[1,1024,256]{2,1,0:T(8,128)} %grad_ref.1, f32[16,128,128]{2,1,0:T(8,128)} %old_ref.1, f32[128,256]{1,0:T(8,128)} %weights_ref.1, ...), custom_call_target="tpu_custom_call" | custom-call | flops 1200000000 | bytes 10000000 | tf_op jit(solution)/shard_map/pallas_call | solution.py:564
  66.7 54.8 %shard_map.95 = (f32[1024,256]{1,0:T(8,128)}, f32[128,256]{1,0:T(8,128)}, f32[9,128,128]{2,1,0:T(8,128)}) custom-call(f32[1024,256]{1,0:T(8,128)} %get-tuple-element.6.weights, f32[128,256]{1,0:T(8,128)} %get-tuple-element.7.momentum, f32[9,128,128]{2,1,0:T(8,128)} %get-tuple-element.8.factors), custom_call_target="tpu_custom_call" | custom-call | bytes 3500000 | tf_op jit(solution)/shard_map/pallas_call | solution.py:617

commit v4 on v3

--- a/solution.py
+++ b/solution.py
@@ -251,9 +251,7 @@
         loads.append(load(gout_ref.at[:, columns], gout_v.at[:, columns], 2 * k + 1))
     weights_load = load(weights_ref, weights_v, 8)
     momentum_load = load(momentum_ref, momentum_v, 9)
-    own_load = load(
-        grad_ref.at[0, pl.ds(pl.multiple_of(s * half, half), half)], grad_own, 10
-    )
+    grad_load = load(grad_ref.at[0], grad_own, 10)
     old_load = load(old_ref, old_v, 11)
 
     rows = lax.broadcasted_iota(jnp.int32, (n, n), 0)
@@ -285,12 +283,9 @@
         if j < 2:
             core_copies.append(send(part(packed_v, start, quarter), core_in.at[j], c_peer))
         if j == 0:
+            grad_load.wait()
             grad_x_copies = [
-                send(
-                    grad_ref.at[0, pl.ds(pl.multiple_of((1 - s) * half + k * n, n), n)],
-                    grad_x.at[k],
-                    x_peer,
-                )
+                send(part(grad_own, (1 - s) * half + k * n, n), grad_x.at[k], x_peer)
                 for k in range(4)
             ]
         elif j == 1:
@@ -323,14 +318,6 @@
     diag_copies = [send(diag_out.at[2], diag_xz.at[place], peer) for peer in xz_peers]
     xz_in[place] = xz_out[place]
     diag_xz[place] = diag
-    own_load.wait()
-    for k in range(4):
-        grad_x_copies[k].wait()
-        grad_x[k] = grad_x[k] + grad_own[pl.ds(k * n, n), :]
-    grad_copies = [
-        send(grad_x.at[q], grad_z.at[r], peer) for q, peer in zip(z_ranks, z_peers)
-    ]
-    grad_z[r] = grad_x[r]
     for copy in copies:
         copy.wait()
     start = pl.multiple_of(starts[3] + place * 32, 32)
@@ -367,6 +354,14 @@
     region = part(full_v, starts[3], quarter)
     y_copy = send(region, region, y_peer)
     core_copies = [send(region, region, c_peer)]
+    for k in range(4):
+        grad_x_copies[k].wait()
+        own_rows = pl.ds(pl.multiple_of(s * half + k * n, n), n)
+        grad_x[k] = grad_x[k] + grad_own[own_rows, :]
+    grad_copies = [
+        send(grad_x.at[q], grad_z.at[r], peer) for q, peer in zip(z_ranks, z_peers)
+    ]
+    grad_z[r] = grad_x[r]
     for copy in base_copies:
         copy.wait()
     region = part(base_all, s * half, half)
@@ -536,21 +531,29 @@
     weights_out[...] = base_all[...] - (step_rate * clip_scale) * precond_all[...]
 
 
-def copy_out_kernel(weights, momentum, factors, weights_out, momentum_out, factors_out, sems):
-    copies = []
-    for src, dst, parts in (
-        (weights, weights_out, 4),
-        (factors, factors_out, 3),
-        (momentum, momentum_out, 1),
+def copy_out_kernel(
+    weights, momentum, factors, weights_out, momentum_out, factors_out, *held_and_sems
+):
+    held, (loads, stores) = held_and_sems[:3], held_and_sems[3:]
+    pieces = []
+    for src, mid, dst, parts in (
+        (weights, held[0], weights_out, 4),
+        (factors, held[2], factors_out, 3),
+        (momentum, held[1], momentum_out, 1),
     ):
         size = src.shape[0] // parts
         for k in range(parts):
             span = pl.ds(k * size, size)
-            copy = pltpu.make_async_copy(src.at[span], dst.at[span], sems.at[len(copies)])
-            copy.start()
-            copies.append(copy)
-    for copy in copies:
-        copy.wait()
+            index = len(pieces)
+            first = pltpu.make_async_copy(src.at[span], mid.at[span], loads.at[index])
+            first.start()
+            second = pltpu.make_async_copy(mid.at[span], dst.at[span], stores.at[index])
+            pieces.append((first, second))
+    for first, second in pieces:
+        first.wait()
+        second.start()
+    for _, second in pieces:
+        second.wait()
 
 
 def fused_step(activations, grads_out, grad_parts, old_factors, block_owner, weights, momentum):
@@ -594,7 +597,7 @@
             pltpu.VMEM((4, 8, n), f32),
             pltpu.VMEM((2, 8, n), f32),
             pltpu.VMEM((8, 8, n), f32),
-            pltpu.VMEM((512, 256), f32),
+            pltpu.VMEM((1024, 256), f32),
             pltpu.VMEM((4, n, 256), f32),
             pltpu.VMEM((4, n, 256), f32),
             pltpu.VMEM((2, 8, n), f32),
@@ -619,7 +622,9 @@
         out_shape=tuple(jax.ShapeDtypeStruct(a.shape, a.dtype) for a in results),
         in_specs=[anywhere] * 3,
         out_specs=(anywhere,) * 3,
-        scratch_shapes=[pltpu.SemaphoreType.DMA((8,))],
+        scratch_shapes=[pltpu.VMEM(a.shape, a.dtype) for a in results]
+        + [pltpu.SemaphoreType.DMA((8,))] * 2,
+        compiler_params=pltpu.CompilerParams(vmem_limit_bytes=60 * 1024 * 1024),
         cost_estimate=pl.CostEstimate(flops=0, bytes_accessed=3_500_000, transcendentals=0),
     )(*results)
 

time: 122 us -> 63.4 us (0.52)
  Pallas kernels: 121 us -> 62.6 us
    pallas_call x1, Pallas kernels: 54.8 us -> 2.28 us  [fused_step(): pl.pallas_call(copy_out_kernel, out_shape=tuple((jax.ShapeDtypeStruct(a.s...]
    pallas_call x1, Pallas kernels: 66 us -> 60.3 us  [fused_step(): pl.pallas_call(functools.partial(fused_kernel, float(activations.shape[0]...]
where the time goes in v4:
time: 63.4 us; the launch traced here: 63.2 us
  Pallas kernels  62.6 us (99%)
  between operations  0.64 us (1%)
    pallas_call x1, Pallas kernels, fused_step(): pl.pallas_call(functools.partial(fused_kernel, float(activations.shape[0]...  60.3 us
    pallas_call x1, Pallas kernels, fused_step(): pl.pallas_call(copy_out_kernel, out_shape=tuple((jax.ShapeDtypeStruct(a.s...  2.28 us

profile of v4, /device:TPU:0, one launch (start us, length us, event | category | flops | bytes accessed | tf_op | source)
XLA Modules:
  0.0 63.2 jit_solution(5256131600874158469)
XLA Ops:
  0.6 60.3 %shard_map.94 = (f32[1024,256]{1,0:T(8,128)}, f32[128,256]{1,0:T(8,128)}, f32[9,128,128]{2,1,0:T(8,128)}) custom-call(s32[16]{0:T(128)} %owner_ref.1, bf16[1024,1024]{1,0:T(8,128)(2,1)} %act_ref.1, bf16[1024,1024]{1,0:T(8,128)(2,1)} %gout_ref.1, f32[1,1024,256]{2,1,0:T(8,128)} %grad_ref.1, f32[16,128,128]{2,1,0:T(8,128)} %old_ref.1, f32[128,256]{1,0:T(8,128)} %weights_ref.1, ...), custom_call_target="tpu_custom_call" | custom-call | flops 1200000000 | bytes 10000000 | tf_op jit(solution)/shard_map/pallas_call | solution.py:567
  60.9 2.3 %shard_map.95 = (f32[1024,256]{1,0:T(8,128)}, f32[128,256]{1,0:T(8,128)}, f32[9,128,128]{2,1,0:T(8,128)}) custom-call(f32[1024,256]{1,0:T(8,128)} %get-tuple-element.6.weights, f32[128,256]{1,0:T(8,128)} %get-tuple-element.7.momentum, f32[9,128,128]{2,1,0:T(8,128)} %get-tuple-element.8.factors), custom_call_target="tpu_custom_call" | custom-call | bytes 3500000 | tf_op jit(solution)/shard_map/pallas_call | solution.py:620

commit v5 on v4

--- a/solution.py
+++ b/solution.py
@@ -196,8 +196,7 @@
     sum_out,
     sum_xz,
     sum_tensor,
-    base_all,
-    precond_all,
+    weights_all,
     mixed_v,
     local_sem,
     sends,
@@ -285,16 +284,9 @@
         if j == 0:
             grad_load.wait()
             grad_x_copies = [
-                send(part(grad_own, (1 - s) * half + k * n, n), grad_x.at[k], x_peer)
-                for k in range(4)
+                send(part(grad_own, (1 - s) * half + q * n, n), grad_x.at[q], x_peer)
+                for q in z_ranks + [r]
             ]
-        elif j == 1:
-            weights_load.wait()
-            momentum_load.wait()
-            own_rows = pl.ds(pl.multiple_of(place * n, n), n)
-            base_all[own_rows, :] = weights_v[...] - (step_rate * momentum_rate) * momentum_v[...]
-            base_own = part(base_all, place * n, n)
-            base_copies = [send(base_own, base_own, peer) for peer in z_peers]
         elif j == 2:
             core_copies[0].wait()
             packed_v[pl.ds(start, quarter), :] += core_in[0]
@@ -312,18 +304,30 @@
     copies = [
         send(xz_out.at[q], xz_in.at[place], peer) for q, peer in zip(xz_places, xz_peers)
     ]
+
+    def add_gradient(k):
+        q = (z_ranks + [r])[k]
+        grad_x_copies[k].wait()
+        grad_x[q] = grad_x[q] + grad_own[pl.ds(pl.multiple_of(s * half + q * n, n), n), :]
+        if k < 3:
+            grad_copies.append(send(grad_x.at[q], grad_z.at[r], z_peers[k]))
+
+    grad_copies = []
     diag_copy.wait()
     diag = diag + diag_in[1]
     diag_out[2] = diag
     diag_copies = [send(diag_out.at[2], diag_xz.at[place], peer) for peer in xz_peers]
     xz_in[place] = xz_out[place]
     diag_xz[place] = diag
+    add_gradient(0)
     for copy in copies:
         copy.wait()
     start = pl.multiple_of(starts[3] + place * 32, 32)
     full_v[pl.ds(start, 32), :] = ordered_sum(xz_in, 8)
     region = part(full_v, start, 32)
     copies = [send(region, region, peer) for peer in xz_peers]
+    add_gradient(1)
+    add_gradient(2)
     for copy in diag_copies:
         copy.wait()
     diag_out[3] = ordered_sum(diag_xz, 8)
@@ -354,18 +358,8 @@
     region = part(full_v, starts[3], quarter)
     y_copy = send(region, region, y_peer)
     core_copies = [send(region, region, c_peer)]
-    for k in range(4):
-        grad_x_copies[k].wait()
-        own_rows = pl.ds(pl.multiple_of(s * half + k * n, n), n)
-        grad_x[k] = grad_x[k] + grad_own[own_rows, :]
-    grad_copies = [
-        send(grad_x.at[q], grad_z.at[r], peer) for q, peer in zip(z_ranks, z_peers)
-    ]
+    add_gradient(3)
     grad_z[r] = grad_x[r]
-    for copy in base_copies:
-        copy.wait()
-    region = part(base_all, s * half, half)
-    base_copy = send(region, region, x_peer)
 
     def blend(pair, packed=None):
         if packed is None:
@@ -422,16 +416,13 @@
 
     sum_out[0] = tile
     sum_copies = [send(sum_out.at[0], sum_xz.at[place], peer) for peer in xz_peers]
-    precond_all[pl.ds(pl.multiple_of(place * n, n), n), :] = precond
-    own = part(precond_all, place * n, n)
-    x_copies = [send(own, own, x_peer)]
 
     first_sem = used_sems[0]
     used_sems[0] += 14
 
     def passing(hop, way, peer, hand_on):
         origin = r - hop if way == 0 else r + hop
-        region = part(precond_all, (s * 4 + origin) * n, n)
+        region = part(weights_all, (s * 4 + origin) * n, n)
         index = first_sem + 6 * hand_on + 2 * hop + way
         return remote(region, region, sends, recvs, index, peer)
 
@@ -457,7 +448,7 @@
             def _():
                 back = ways[1 - way]
                 origin = r - hop - 1 if way == 0 else r + hop + 1
-                region = part(precond_all, (s * 4 + origin) * n, n)
+                region = part(weights_all, (s * 4 + origin) * n, n)
                 index = first_sem + 2 * hop + way
                 remote(region, region, sends, recvs, index, back).wait_recv()
 
@@ -468,7 +459,6 @@
             def _():
                 passing(hop + 1, way, x_peer, 1).start()
 
-    start_hop(0)
     sum_xz[place] = tile
     for copy in sum_copies:
         copy.wait()
@@ -478,14 +468,23 @@
         send(sum_out.at[1], sum_tensor.at[t], peer) for peer in (c_peer, y_peer, yc_peer)
     ]
     sum_tensor[t] = tile
+    weights_load.wait()
+    momentum_load.wait()
+    for copy in sum_copies:
+        copy.wait()
+    alignment = jnp.sum(ordered_sum(sum_tensor, 4), keepdims=True)
+    clip_scale = jnp.minimum(1.0, clip_norm / jnp.sqrt(alignment))
+    momentum_next = momentum_rate * momentum_v[...] + clip_scale * precond
+    weights_all[pl.ds(pl.multiple_of(place * n, n), n), :] = (
+        weights_v[...] - step_rate * momentum_next
+    )
+    own = part(weights_all, place * n, n)
+    x_copies = [send(own, own, x_peer)]
+    start_hop(0)
+    momentum_out[...] = momentum_next
     arrived(0)
     start_hop(1)
     hand_on(0)
-    for copy in sum_copies:
-        copy.wait()
-    alignment = jnp.sum(ordered_sum(sum_tensor, 4), keepdims=True)
-    clip_scale = jnp.minimum(1.0, clip_norm / jnp.sqrt(alignment))
-    momentum_out[...] = momentum_rate * momentum_v[...] + clip_scale * precond
     arrived(1)
     start_hop(2)
     hand_on(1)
@@ -514,7 +513,6 @@
 
     arrived(2)
     hand_on(2)
-    base_copy.wait()
     for copy in x_copies:
         copy.wait()
     for hop in range(3):
@@ -528,7 +526,7 @@
             def _():
                 passing(hop + 1, way, x_peer, 1).wait()
 
-    weights_out[...] = base_all[...] - (step_rate * clip_scale) * precond_all[...]
+    weights_out[...] = weights_all[...]
 
 
 def copy_out_kernel(
@@ -604,7 +602,6 @@
             pltpu.VMEM((8, 8, n), f32),
             pltpu.VMEM((4, 8, n), f32),
             pltpu.VMEM((1024, 256), f32),
-            pltpu.VMEM((1024, 256), f32),
             pltpu.VMEM((17, n, n), f32),
             pltpu.SemaphoreType.DMA((12,)),
             pltpu.SemaphoreType.DMA((72,)),

time: 63.4 us -> 65.3 us (1.030)
  Pallas kernels: 62.6 us -> 64.6 us
    pallas_call x1, Pallas kernels: 60.3 us -> 62.3 us  [fused_step(): pl.pallas_call(functools.partial(fused_kernel, float(activations.shape[0]...]
where the time goes in v5:
time: 65.3 us; the launch traced here: 65.2 us
  Pallas kernels  64.6 us (99%)
    pallas_call x1, Pallas kernels, fused_step(): pl.pallas_call(functools.partial(fused_kernel, float(activations.shape[0]...  62.3 us
    pallas_call x1, Pallas kernels, fused_step(): pl.pallas_call(copy_out_kernel, out_shape=tuple((jax.ShapeDtypeStruct(a.s...  2.28 us

profile of v5, /device:TPU:0, one launch (start us, length us, event | category | flops | bytes accessed | tf_op | source)
XLA Modules:
  0.0 65.2 jit_solution(14975735655850891990)
XLA Ops:
  0.6 62.3 %shard_map.94 = (f32[1024,256]{1,0:T(8,128)}, f32[128,256]{1,0:T(8,128)}, f32[9,128,128]{2,1,0:T(8,128)}) custom-call(s32[16]{0:T(128)} %owner_ref.1, bf16[1024,1024]{1,0:T(8,128)(2,1)} %act_ref.1, bf16[1024,1024]{1,0:T(8,128)(2,1)} %gout_ref.1, f32[1,1024,256]{2,1,0:T(8,128)} %grad_ref.1, f32[16,128,128]{2,1,0:T(8,128)} %old_ref.1, f32[128,256]{1,0:T(8,128)} %weights_ref.1, ...), custom_call_target="tpu_custom_call" | custom-call | flops 1200000000 | bytes 10000000 | tf_op jit(solution)/shard_map/pallas_call | solution.py:565
  62.9 2.3 %shard_map.95 = (f32[1024,256]{1,0:T(8,128)}, f32[128,256]{1,0:T(8,128)}, f32[9,128,128]{2,1,0:T(8,128)}) custom-call(f32[1024,256]{1,0:T(8,128)} %get-tuple-element.6.weights, f32[128,256]{1,0:T(8,128)} %get-tuple-element.7.momentum, f32[9,128,128]{2,1,0:T(8,128)} %get-tuple-element.8.factors), custom_call_target="tpu_custom_call" | custom-call | bytes 3500000 | tf_op jit(solution)/shard_map/pallas_call | solution.py:617

commit v6 on v4

--- a/solution.py
+++ b/solution.py
@@ -285,8 +285,8 @@
         if j == 0:
             grad_load.wait()
             grad_x_copies = [
-                send(part(grad_own, (1 - s) * half + k * n, n), grad_x.at[k], x_peer)
-                for k in range(4)
+                send(part(grad_own, (1 - s) * half + q * n, n), grad_x.at[q], x_peer)
+                for q in z_ranks + [r]
             ]
         elif j == 1:
             weights_load.wait()
@@ -312,6 +312,15 @@
     copies = [
         send(xz_out.at[q], xz_in.at[place], peer) for q, peer in zip(xz_places, xz_peers)
     ]
+
+    def add_gradient(k):
+        q = (z_ranks + [r])[k]
+        grad_x_copies[k].wait()
+        grad_x[q] = grad_x[q] + grad_own[pl.ds(pl.multiple_of(s * half + q * n, n), n), :]
+        if k < 3:
+            grad_copies.append(send(grad_x.at[q], grad_z.at[r], z_peers[k]))
+
+    grad_copies = []
     diag_copy.wait()
     diag = diag + diag_in[1]
     diag_out[2] = diag
@@ -324,6 +333,8 @@
     full_v[pl.ds(start, 32), :] = ordered_sum(xz_in, 8)
     region = part(full_v, start, 32)
     copies = [send(region, region, peer) for peer in xz_peers]
+    add_gradient(0)
+    add_gradient(1)
     for copy in diag_copies:
         copy.wait()
     diag_out[3] = ordered_sum(diag_xz, 8)
@@ -354,13 +365,8 @@
     region = part(full_v, starts[3], quarter)
     y_copy = send(region, region, y_peer)
     core_copies = [send(region, region, c_peer)]
-    for k in range(4):
-        grad_x_copies[k].wait()
-        own_rows = pl.ds(pl.multiple_of(s * half + k * n, n), n)
-        grad_x[k] = grad_x[k] + grad_own[own_rows, :]
-    grad_copies = [
-        send(grad_x.at[q], grad_z.at[r], peer) for q, peer in zip(z_ranks, z_peers)
-    ]
+    add_gradient(2)
+    add_gradient(3)
     grad_z[r] = grad_x[r]
     for copy in base_copies:
         copy.wait()

time: 63.4 us -> 61.3 us (0.967)
  Pallas kernels: 62.6 us -> 60.5 us
    pallas_call x1, Pallas kernels: 60.3 us -> 58.2 us  [fused_step(): pl.pallas_call(functools.partial(fused_kernel, float(activations.shape[0]...]
where the time goes in v6:
time: 61.3 us; the launch traced here: 61.1 us
  Pallas kernels  60.5 us (99%)
  between operations  0.64 us (1%)
    pallas_call x1, Pallas kernels, fused_step(): pl.pallas_call(functools.partial(fused_kernel, float(activations.shape[0]...  58.2 us
    pallas_call x1, Pallas kernels, fused_step(): pl.pallas_call(copy_out_kernel, out_shape=tuple((jax.ShapeDtypeStruct(a.s...  2.28 us

profile of v6, /device:TPU:0, one launch (start us, length us, event | category | flops | bytes accessed | tf_op | source)
XLA Modules:
  0.0 61.1 jit_solution(4129485037432492244)
XLA Ops:
  0.6 58.2 %shard_map.94 = (f32[1024,256]{1,0:T(8,128)}, f32[128,256]{1,0:T(8,128)}, f32[9,128,128]{2,1,0:T(8,128)}) custom-call(s32[16]{0:T(128)} %owner_ref.1, bf16[1024,1024]{1,0:T(8,128)(2,1)} %act_ref.1, bf16[1024,1024]{1,0:T(8,128)(2,1)} %gout_ref.1, f32[1,1024,256]{2,1,0:T(8,128)} %grad_ref.1, f32[16,128,128]{2,1,0:T(8,128)} %old_ref.1, f32[128,256]{1,0:T(8,128)} %weights_ref.1, ...), custom_call_target="tpu_custom_call" | custom-call | flops 1200000000 | bytes 10000000 | tf_op jit(solution)/shard_map/pallas_call | solution.py:573
  58.8 2.3 %shard_map.95 = (f32[1024,256]{1,0:T(8,128)}, f32[128,256]{1,0:T(8,128)}, f32[9,128,128]{2,1,0:T(8,128)}) custom-call(f32[1024,256]{1,0:T(8,128)} %get-tuple-element.6.weights, f32[128,256]{1,0:T(8,128)} %get-tuple-element.7.momentum, f32[9,128,128]{2,1,0:T(8,128)} %get-tuple-element.8.factors), custom_call_target="tpu_custom_call" | custom-call | bytes 3500000 | tf_op jit(solution)/shard_map/pallas_call | solution.py:626

commit v7 on v6

--- a/solution.py
+++ b/solution.py
@@ -335,6 +335,7 @@
     copies = [send(region, region, peer) for peer in xz_peers]
     add_gradient(0)
     add_gradient(1)
+    add_gradient(2)
     for copy in diag_copies:
         copy.wait()
     diag_out[3] = ordered_sum(diag_xz, 8)
@@ -365,7 +366,6 @@
     region = part(full_v, starts[3], quarter)
     y_copy = send(region, region, y_peer)
     core_copies = [send(region, region, c_peer)]
-    add_gradient(2)
     add_gradient(3)
     grad_z[r] = grad_x[r]
     for copy in base_copies:
@@ -520,6 +520,13 @@
 
     arrived(2)
     hand_on(2)
+
+    def finish(side):
+        span = pl.ds(pl.multiple_of(side * half, half), half)
+        step_scale = step_rate * clip_scale
+        weights_out[span, :] = base_all[span, :] - step_scale * precond_all[span, :]
+
+    finish(s)
     base_copy.wait()
     for copy in x_copies:
         copy.wait()
@@ -534,7 +541,7 @@
             def _():
                 passing(hop + 1, way, x_peer, 1).wait()
 
-    weights_out[...] = base_all[...] - (step_rate * clip_scale) * precond_all[...]
+    finish(1 - s)
 
 
 def copy_out_kernel(

time: 61.3 us -> 61.3 us (level)
  no operation moved by 1% of the time
where the time goes in v7:
time: 61.3 us; the launch traced here: 61.1 us
  Pallas kernels  60.5 us (99%)
  between operations  0.64 us (1%)
    pallas_call x1, Pallas kernels, fused_step(): pl.pallas_call(functools.partial(fused_kernel, float(activations.shape[0]...  58.2 us
    pallas_call x1, Pallas kernels, fused_step(): pl.pallas_call(copy_out_kernel, out_shape=tuple((jax.ShapeDtypeStruct(a.s...  2.28 us

profile of v7, /device:TPU:0, one launch (start us, length us, event | category | flops | bytes accessed | tf_op | source)
XLA Modules:
  0.0 61.1 jit_solution(13062461100424094048)
XLA Ops:
  0.6 58.2 %shard_map.94 = (f32[1024,256]{1,0:T(8,128)}, f32[128,256]{1,0:T(8,128)}, f32[9,128,128]{2,1,0:T(8,128)}) custom-call(s32[16]{0:T(128)} %owner_ref.1, bf16[1024,1024]{1,0:T(8,128)(2,1)} %act_ref.1, bf16[1024,1024]{1,0:T(8,128)(2,1)} %gout_ref.1, f32[1,1024,256]{2,1,0:T(8,128)} %grad_ref.1, f32[16,128,128]{2,1,0:T(8,128)} %old_ref.1, f32[128,256]{1,0:T(8,128)} %weights_ref.1, ...), custom_call_target="tpu_custom_call" | custom-call | flops 1200000000 | bytes 10000000 | tf_op jit(solution)/shard_map/pallas_call | solution.py:580
  58.8 2.3 %shard_map.95 = (f32[1024,256]{1,0:T(8,128)}, f32[128,256]{1,0:T(8,128)}, f32[9,128,128]{2,1,0:T(8,128)}) custom-call(f32[1024,256]{1,0:T(8,128)} %get-tuple-element.6.weights, f32[128,256]{1,0:T(8,128)} %get-tuple-element.7.momentum, f32[9,128,128]{2,1,0:T(8,128)} %get-tuple-element.8.factors), custom_call_target="tpu_custom_call" | custom-call | bytes 3500000 | tf_op jit(solution)/shard_map/pallas_call | solution.py:633

commit v8 on v7

--- a/solution.py
+++ b/solution.py
@@ -327,13 +327,13 @@
     diag_copies = [send(diag_out.at[2], diag_xz.at[place], peer) for peer in xz_peers]
     xz_in[place] = xz_out[place]
     diag_xz[place] = diag
+    add_gradient(0)
     for copy in copies:
         copy.wait()
     start = pl.multiple_of(starts[3] + place * 32, 32)
     full_v[pl.ds(start, 32), :] = ordered_sum(xz_in, 8)
     region = part(full_v, start, 32)
     copies = [send(region, region, peer) for peer in xz_peers]
-    add_gradient(0)
     add_gradient(1)
     add_gradient(2)
     for copy in diag_copies:

time: 61.3 us -> 67.1 us (1.095)
  Pallas kernels: 60.5 us -> 66.3 us
    pallas_call x1, Pallas kernels: 58.2 us -> 64 us  [fused_step(): pl.pallas_call(functools.partial(fused_kernel, float(activations.shape[0]...]
where the time goes in v8:
time: 67.1 us; the launch traced here: 67 us
  Pallas kernels  66.3 us (99%)
    pallas_call x1, Pallas kernels, fused_step(): pl.pallas_call(functools.partial(fused_kernel, float(activations.shape[0]...  64 us
    pallas_call x1, Pallas kernels, fused_step(): pl.pallas_call(copy_out_kernel, out_shape=tuple((jax.ShapeDtypeStruct(a.s...  2.28 us

profile of v8, /device:TPU:0, one launch (start us, length us, event | category | flops | bytes accessed | tf_op | source)
XLA Modules:
  0.0 67.0 jit_solution(8449573929166774925)
XLA Ops:
  0.6 64.0 %shard_map.94 = (f32[1024,256]{1,0:T(8,128)}, f32[128,256]{1,0:T(8,128)}, f32[9,128,128]{2,1,0:T(8,128)}) custom-call(s32[16]{0:T(128)} %owner_ref.1, bf16[1024,1024]{1,0:T(8,128)(2,1)} %act_ref.1, bf16[1024,1024]{1,0:T(8,128)(2,1)} %gout_ref.1, f32[1,1024,256]{2,1,0:T(8,128)} %grad_ref.1, f32[16,128,128]{2,1,0:T(8,128)} %old_ref.1, f32[128,256]{1,0:T(8,128)} %weights_ref.1, ...), custom_call_target="tpu_custom_call" | custom-call | flops 1200000000 | bytes 10000000 | tf_op jit(solution)/shard_map/pallas_call | solution.py:580
  64.7 2.3 %shard_map.95 = (f32[1024,256]{1,0:T(8,128)}, f32[128,256]{1,0:T(8,128)}, f32[9,128,128]{2,1,0:T(8,128)}) custom-call(f32[1024,256]{1,0:T(8,128)} %get-tuple-element.6.weights, f32[128,256]{1,0:T(8,128)} %get-tuple-element.7.momentum, f32[9,128,128]{2,1,0:T(8,128)} %get-tuple-element.8.factors), custom_call_target="tpu_custom_call" | custom-call | bytes 3500000 | tf_op jit(solution)/shard_map/pallas_call | solution.py:633
